TPU v7x, 512 devices: a whole 4x4x16 slice. The times are simulated.
512 devices in a mesh: batch: 64 (over z, y_lo, core), tensor: 8 (over x, y_hi).
Axes of the slice: x: 4, y: 4 (y_hi: 2, y_lo: 2; y = y_hi * 2 + y_lo), z: 16, core: 2. Of those that a mesh axis runs over, the one named last changes fastest.
Arguments:
- image_student: bfloat16 [12288, 512], P('batch', 'tensor'), may hold values from -64 to 64
- text_student: bfloat16 [12288, 512], P(('batch', 'tensor')), may hold values from -4 to 4
- image_teacher: bfloat16 [12288, 1280], P('batch'), may hold values from -64 to 64
- text_teacher: bfloat16 [12288, 1280], P(('batch', 'tensor')), may hold values from -4 to 4
- student_scale: float32 [1], replicated, may hold values from 1.5 to 3
- teacher_scale: float32 [1], replicated, may hold values from 1.5 to 3
Outputs:
- pair_loss: float32 [12288], P(('batch', 'tensor'))
- grad_image: float32 [12288, 512], P('batch', 'tensor')
- grad_text: float32 [12288, 512], P(('batch', 'tensor'))
All inputs are finite; a program needn't handle non-finite values.
Results may differ from a plain program's by a relative error of at most 0.0065.
Values may be sent and summed in bfloat16 or wider, within the bound.
A program may use at most 64 MiB of HBM per device.

v0:
```python
import jax
import jax.numpy as jnp
from jax import lax
from jax.sharding import PartitionSpec as P


def local_scores(image_rows, teacher_rows, piece, factors):
    width = image_rows.shape[1]
    contract = (((1,), (1,)), ((), ()))
    student = (
        lax.dot_general(image_rows, piece[:, :width], contract, preferred_element_type=jnp.float32)
        * factors[0]
    )
    teacher = (
        lax.dot_general(
            teacher_rows, piece[:, width:], contract, preferred_element_type=jnp.float32
        )
        * factors[1]
    )
    return (student, teacher)


def tile_stats(student, teacher, axis):
    peak = jnp.stack([jnp.max(student, axis), jnp.max(teacher, axis)])
    teacher_weights = jnp.exp(teacher - jnp.expand_dims(peak[1], axis))
    sums = jnp.stack(
        [
            jnp.sum(jnp.exp(student - jnp.expand_dims(peak[0], axis)), axis),
            jnp.sum(teacher_weights, axis),
        ]
    )
    weighted = jnp.sum(teacher_weights * student, axis)
    return (peak, sums, weighted)


def grad_tile(student, teacher, row_lse, col_lse):
    grads = 0.5 * (
        jnp.exp(student - row_lse[0][:, None])
        - jnp.exp(teacher - row_lse[1][:, None])
        + jnp.exp(student - col_lse[0][None, :])
        - jnp.exp(teacher - col_lse[1][None, :])
    )
    return grads.astype(jnp.bfloat16)


def body(image_student, text_student, image_teacher, text_teacher, student_scale, teacher_scale):
    pairs = text_student.shape[0]
    width = text_student.shape[1]
    factors = (
        student_scale[0] / jnp.sqrt(jnp.float32(width)),
        teacher_scale[0] / jnp.sqrt(jnp.float32(text_teacher.shape[1])),
    )
    image_rows = lax.all_gather(image_student, "tensor", axis=1, tiled=True)
    texts = jnp.concatenate([text_student, text_teacher], 1)
    transpose_contract = (((0,), (0,)), ((), ()))
    gathered = lax.all_gather(texts, "batch", axis=0, tiled=True)
    student, teacher = local_scores(image_rows, image_teacher, gathered, factors)
    row_local = tile_stats(student, teacher, 1)
    col_local = tile_stats(student, teacher, 0)
    row_peak = lax.pmax(row_local[0], "tensor")
    col_peak = lax.pmax(col_local[0], "batch")
    row_factor = jnp.exp(row_local[0] - row_peak)
    col_factor = jnp.exp(col_local[0] - col_peak)
    row_sums, row_weighted = lax.psum(
        (row_local[1] * row_factor, row_local[2] * row_factor[1]), "tensor"
    )
    col_sums, col_weighted = lax.psum(
        (col_local[1] * col_factor, col_local[2] * col_factor[1]), "batch"
    )
    row_lse = row_peak + jnp.log(row_sums)
    col_lse = col_peak + jnp.log(col_sums)
    row_loss = row_lse[0] - row_weighted / row_sums[1]
    col_loss = col_lse[0] - col_weighted / col_sums[1]
    tensor_index = lax.axis_index("tensor")
    batch_index = lax.axis_index("batch")
    pair_loss = 0.5 * (
        lax.dynamic_slice_in_dim(row_loss, tensor_index * pairs, pairs)
        + lax.dynamic_slice_in_dim(col_loss, batch_index * pairs, pairs)
    )
    grads = grad_tile(student, teacher, row_lse, col_lse)
    image_term = (
        jnp.dot(grads, gathered[:, :width], preferred_element_type=jnp.float32) * factors[0]
    )
    grad_text = lax.psum_scatter(
        lax.dot_general(grads, image_rows, transpose_contract, preferred_element_type=jnp.float32)
        * factors[0],
        "batch",
        scatter_dimension=0,
        tiled=True,
    )
    grad_image = lax.psum_scatter(image_term, "tensor", scatter_dimension=1, tiled=True)
    return (pair_loss, grad_image, grad_text)


def solution(mesh):
    return jax.shard_map(
        body,
        mesh=mesh,
        in_specs=(
            P("batch", "tensor"),
            P(("batch", "tensor"), None),
            P("batch", None),
            P(("batch", "tensor"), None),
            P(),
            P(),
        ),
        out_specs=(P(("batch", "tensor")), P("batch", "tensor"), P(("batch", "tensor"), None)),
        check_vma=False,
    )
```

profile of v0, /device:TPU:1, one launch (start us, length us, event | category | flops | bytes accessed | tf_op | source)
XLA Modules:
  0.0 927.4 jit_solution(10153787075987626962)
XLA Ops:
  7.2 0.0 copy-start
  7.2 0.0 all-gather.2.cloned.1.call-start
  7.2 1.5 pad_maximum_fusion
  8.7 0.0 all-gather.2.cloned.1.call-update
  8.8 0.0 reduce-scatter.3.cloned.1.call-start
  10.1 29.7 %all_gather.7 = bf16[192,512]{0,1:T(8,128)(2,1)S(1)} all-gather(bf16[192,64]{0,1:T(8,128)(2,1)} %param.6), channel_id=1, replica_groups=mesh['batch'=64,'tensor'=8] {'tensor'}, dimensions={1}, use_global_device_ids=true | all-gather | bytes 221184 | tf_op jit(solution)/shard_map/all_gather | solution.py:53
  39.8 0.0 copy-start.1
  39.8 102.2 %all-gather.2.cloned.1.call-done = bf16[1536,1792]{1,0:T(8,128)(2,1)} async-done(((bf16[24,1792]{1,0:T(8,128)(2,1)}), bf16[1536,1792]{1,0:T(8,128)(2,1)}) %all-gather.2.cloned.1.call-update) | async-done | bytes 5505040 | tf_op jit(solution)/shard_map/all_gather | solution.py:56
  142.0 0.0 copy-done
  142.0 3.6 fusion.16
  145.7 0.0 copy-done.1
  145.7 2.2 fusion.15
  147.9 20.1 %pmax.14 = f32[2,192]{1,0:T(2,128)S(1)} all-reduce(f32[2,192]{1,0:T(2,128)S(1)} %pad_maximum_fusion.2), channel_id=1, replica_groups=mesh['batch'=64,'tensor'=8] {'tensor'}, use_global_device_ids=true, to_apply=%region_2.0 | all-reduce | flops 384 | bytes 3072 | tf_op jit(solution)/shard_map/pmax | solution.py:60
  168.0 1.0 multiply_reduce_fusion.1
  169.1 15.5 %all-reduce.1 = (f32[2,192]{1,0:T(2,128)S(1)}, f32[192]{0:T(256)S(1)}) all-reduce(f32[2,192]{1,0:T(2,128)S(1)} %get-tuple-element.19, f32[192]{0:T(256)S(1)} %mul.67), channel_id=1, replica_groups=mesh['batch'=64,'tensor'=8] {'tensor'}, use_global_device_ids=true, to_apply=%region_5.0 | all-reduce | flops 576 | bytes 4608 | tf_op jit(solution)/shard_map/psum | solution.py:64
  184.7 210.5 %pmax.15 = f32[2,1536]{1,0:T(2,128)S(1)} all-reduce(f32[2,1536]{1,0:T(2,128)S(1)} %pad_maximum_fusion.1), channel_id=1, replica_groups=mesh['batch'=64,'tensor'=8] {'batch'}, use_global_device_ids=true, to_apply=%region_10.0 | all-reduce | flops 3072 | bytes 24576 | tf_op jit(solution)/shard_map/pmax | solution.py:61
  395.2 207.4 %all-reduce = (f32[2,1536]{1,0:T(2,128)S(1)}, f32[1536]{0:T(1024)S(1)}) all-reduce(f32[2,1536]{1,0:T(2,128)S(1)} %get-tuple-element.21, f32[1536]{0:T(1024)S(1)} %mul.71), channel_id=1, replica_groups=mesh['batch'=64,'tensor'=8] {'batch'}, use_global_device_ids=true, to_apply=%region_13.0 | all-reduce | flops 4608 | bytes 36864 | tf_op jit(solution)/shard_map/psum | solution.py:67
  602.7 0.7 multiply_convert_fusion
  603.4 0.0 copy-start.2
  603.4 3.0 fusion.8
  606.5 0.0 reduce-scatter.3.cloned.1.call-update
  606.5 0.0 reduce-scatter.5.cloned.1.call-start
  606.5 0.0 copy-done.2
  606.5 2.3 convolution_multiply_fusion
  608.8 0.0 reduce-scatter.5.cloned.1.call-update
  608.9 0.6 fusion.14
  609.5 79.9 %reduce-scatter.3.cloned.1.call-done = f32[192,64]{0,1:T(8,128)} async-done(((f32[192,512]{0,1:T(8,128)}), f32[192,64]{0,1:T(8,128)}) %reduce-scatter.3.cloned.1.call-update) | async-done | bytes 49168 | tf_op jit(solution)/shard_map/reduce_scatter | solution.py:91
  689.4 231.4 %reduce-scatter.5.cloned.1.call-done = f32[24,512]{1,0:T(8,128)} async-done(((f32[1536,512]{1,0:T(8,128)}), f32[24,512]{1,0:T(8,128)}) %reduce-scatter.5.cloned.1.call-update) | async-done | bytes 49168 | tf_op jit(solution)/shard_map/reduce_scatter | solution.py:84
  (19 shorter events, 0.2 us)
Async XLA Ops:
  7.2 134.9 %copy-start = (bf16[192,1280]{1,0:T(8,128)(2,1)S(1)}, bf16[192,1280]{1,0:T(8,128)(2,1)}, u32[]{:S(2)}) copy-start(bf16[192,1280]{1,0:T(8,128)(2,1)} %param.8) | copy-start | bytes 1474564
  7.2 134.9 %all-gather.2.cloned.1.call-start = ((), (), s32[]{:S(2)}) async-start(), calls=%async_computation.2 | async-start | bytes 5591040 | tf_op jit(solution)/shard_map/all_gather | solution.py:56
  8.8 680.6 %reduce-scatter.3.cloned.1.call-start = ((), (), s32[]{:S(2)}) async-start(), calls=%async_computation.3 | async-start | bytes 589824 | tf_op jit(solution)/shard_map/reduce_scatter | solution.py:91
  39.8 105.9 %copy-start.1 = (bf16[192,512]{0,1:T(8,128)(2,1)}, bf16[192,512]{0,1:T(8,128)(2,1)S(1)}, u32[]{:S(2)}) copy-start(bf16[192,512]{0,1:T(8,128)(2,1)S(1)} %all_gather.7) | copy-start | bytes 589828
  603.4 3.1 copy-start.2
  606.5 314.4 %reduce-scatter.5.cloned.1.call-start = ((), (), s32[]{:S(2)}) async-start(), calls=%async_computation.4 | async-start | bytes 3194880 | tf_op jit(solution)/shard_map/reduce_scatter | solution.py:84
Sparse Core Ops, SparseCore 0:
  10.2 131.8 all-gather.1
  606.6 82.7 reduce-scatter.2
  693.0 227.7 reduce-scatter.4
where the time goes:
time: 931 us; the launch traced here: 927 us
  blocking collectives  483 us (52%)
  waiting for transfers between devices  414 us (44%)
  between operations  15.2 us (2%)
  matrix products  11.1 us (1%)
    reduce_scatter x1, waiting for transfers between devices, body(): lax.psum_scatter(lax.dot_general(grads, image_rows, transpose_contract, p...  231 us
    pmax x1, blocking collectives, body(): col_peak = lax.pmax(col_local[0], 'batch')  210 us
    psum x1, blocking collectives, body(): lax.psum((col_local[1] * col_factor, col_local[2] * col_factor[1]), 'batch')  207 us
    all_gather x1, waiting for transfers between devices, body(): gathered = lax.all_gather(texts, 'batch', axis=0, tiled=True)  102 us
    reduce_scatter x1, waiting for transfers between devices, body(): lax.psum_scatter(image_term, 'tensor', scatter_dimension=1, tiled=True)  79.9 us
    all_gather x1, blocking collectives, body(): image_rows = lax.all_gather(image_student, 'tensor', axis=1, tiled=True)  29.7 us
    pmax x1, blocking collectives, body(): row_peak = lax.pmax(row_local[0], 'tensor')  20.1 us
  transfers between devices with their start and end apart: 3, of which 3 were waited for; matrix products, arithmetic and copies ran while one was open for 0% of the time, Pallas kernels for 0%

commit v1 on v0

v1 whole, which is shorter than its diff:
```python
import functools

import jax
import jax.numpy as jnp
from jax import lax
from jax.experimental import pallas as pl
from jax.experimental.pallas import tpu as pltpu
from jax.sharding import PartitionSpec as P

MESH = pl.DeviceIdType.MESH
F32 = jnp.float32
BF16 = jnp.bfloat16
NT = (((1,), (1,)), ((), ()))


def remote(src, dst, send, recv, device):
    return pltpu.make_async_remote_copy(
        src_ref=src,
        dst_ref=dst,
        send_sem=send,
        recv_sem=recv,
        device_id=device,
        device_id_type=MESH,
    )


def loop(low, high, body):
    def step(i, carry):
        body(i)
        return carry

    lax.fori_loop(low, high, step, 0)


def combine(buf, count, shape):
    row = lax.broadcasted_iota(jnp.int32, shape, 0)
    peak = buf[0]
    for k in range(1, count):
        peak = jnp.maximum(peak, buf[k])
    total = jnp.zeros(shape, F32)
    for k in range(count):
        message = buf[k]
        mean = jnp.broadcast_to(message[3:4], shape)
        total = total + jnp.exp(message - peak) * jnp.where(row == 2, mean, 1.0)
    lse = peak[0:2] + jnp.log(total[0:2])
    loss = lse[0:1] - total[2:3] / total[1:2]
    return lse[0:1], lse[1:2], loss


def kernel(
    zn,
    tn,
    xs_ref,
    xt_ref,
    ts_ref,
    tt_ref,
    ss_ref,
    st_ref,
    loss_ref,
    gi_ref,
    gt_ref,
    buf_s,
    buf_t0,
    buf_t1,
    text_s,
    text_t,
    stu,
    img_s,
    img_t,
    sc_s,
    sc_t,
    e_rs,
    e_rt,
    e_cs,
    e_ct,
    colstat,
    cbuf,
    rbuf,
    colback,
    rowback,
    g_ref,
    gtr_ref,
    q_ref,
    rstage,
    rland,
    istage,
    iland,
    tsend,
    trecv,
    xsend,
    xrecv,
    ssend,
    srecv,
    csend,
    crecv,
    rsend,
    rrecv,
    isend,
    irecv,
    gsend,
    grecv,
):
    pn = 4 * tn
    half = zn // 2
    b = lax.axis_index("batch")
    t = lax.axis_index("tensor")
    z = lax.div(b, 4)
    ylo = lax.rem(lax.div(b, 2), 2)
    core = lax.rem(b, 2)
    yhi = lax.rem(t, 2)
    rb = core * 2 + ylo
    me = rb * tn + t
    rows = xt_ref.shape[0]
    mid = rows // 2
    pairs = ts_ref.shape[0]
    texts = zn * pairs
    images = 4 * rows
    ws = ts_ref.shape[1]
    wt = tt_ref.shape[1]
    wh = wt // 2

    def plane(p):
        r = lax.div(p, tn)
        return (4 * z + lax.rem(r, 2) * 2 + lax.div(r, 2), lax.rem(p, tn))

    def ring(k):
        return (lax.rem(k, zn) * 4 + ylo * 2 + core, t)

    sibling = (b + 1 - 2 * core, t)
    barrier = pltpu.get_barrier_semaphore()

    def greet_plane(d):
        pl.semaphore_signal(
            barrier, inc=1, device_id=plane(lax.rem(me + d, pn)), device_id_type=MESH
        )

    def greet_ring(d):
        pl.semaphore_signal(barrier, inc=1, device_id=ring(z + d), device_id_type=MESH)

    loop(1, zn, greet_ring)
    loop(1, pn, greet_plane)

    bufs = (buf_s, buf_t0, buf_t1)
    buf_s[z] = ts_ref[...]
    buf_t0[z] = tt_ref[:, :wh]
    buf_t1[z] = tt_ref[:, wh:]
    own = xs_ref[...].astype(F32)
    q = ylo * tn + t
    stu[core * 2 * tn + q] = jnp.concatenate([own[:mid], own[mid:]], 1).astype(BF16)

    pl.semaphore_wait(barrier, pn + zn - 2)

    right = ring(z + 1)
    left = ring(z + zn - 1)

    def text_copy(c, way, s):
        if way == 0:
            o = lax.rem(z + zn - s, zn)
        else:
            o = lax.rem(z + s, zn)
        slot = bufs[c].at[o]
        return remote(
            slot, slot, tsend.at[c, way, s], trecv.at[c, way, s], right if way == 0 else left
        )

    def text_wait(c, way, s):
        if way == 0:
            o = lax.rem(z + zn - 1 - s, zn)
        else:
            o = lax.rem(z + 1 + s, zn)
        slot = bufs[c].at[o]
        remote(
            slot, slot, tsend.at[c, way, s], trecv.at[c, way, s], right if way == 0 else left
        ).wait_recv()

    for c in range(3):
        for way in range(2):
            text_copy(c, way, 0).start()

    def block(r, start, size):
        return img_t.at[pl.ds(pl.multiple_of(r * rows + start, mid), size)]

    up = (4 * z + (1 - ylo) * 2 + core, t - yhi + lax.rem(yhi + ylo, 2))
    down = (4 * z + (1 - ylo) * 2 + core, t - yhi + lax.rem(yhi + 1 - ylo, 2))
    other = core * 2 + 1 - ylo
    far = (1 - core) * 2

    def teach(k, src, dst, device):
        return remote(src, dst, xsend.at[k], xrecv.at[k], device)

    to_up = teach(0, xt_ref.at[pl.ds(0, mid)], block(rb, 0, mid), up)
    to_down = teach(1, xt_ref.at[pl.ds(mid, mid)], block(rb, mid, mid), down)
    to_sib = teach(2, xt_ref, block(rb, 0, rows), sibling)
    to_up.start()
    to_down.start()
    to_sib.start()
    img_t[pl.ds(pl.multiple_of(rb * rows, mid), rows)] = xt_ref[...]

    sn = 2 * tn
    own_stu = stu.at[core * sn + q]

    def stu_copy(d):
        p = lax.rem(q + d, sn)
        device = (4 * z + lax.div(p, tn) * 2 + core, lax.rem(p, tn))
        return remote(own_stu, own_stu, ssend.at[d], srecv.at[d], device)

    loop(1, sn, lambda d: stu_copy(d).start())

    def text_step(s):
        for c in range(3):
            for way in range(2):
                text_wait(c, way, s - 1)
                text_copy(c, way, s).start()

    switch = half // 2
    loop(1, switch, text_step)

    def stu_wait(d):
        p = lax.rem(q + sn - d, sn)
        slot = stu.at[core * sn + p]
        remote(slot, slot, ssend.at[d], srecv.at[d], sibling).wait_recv()

    loop(1, sn, stu_wait)
    mine = stu.at[pl.ds(core * sn, sn)]
    stu_sib = remote(mine, mine, ssend.at[0], srecv.at[0], sibling)
    stu_sib.start()
    teach(0, xt_ref.at[pl.ds(0, mid)], block(other, 0, mid), up).wait_recv()
    teach(1, xt_ref.at[pl.ds(mid, mid)], block(other, mid, mid), down).wait_recv()
    to_sib2 = teach(3, block(other, 0, rows), block(other, 0, rows), sibling)
    to_sib2.start()

    loop(switch, half - 1, text_step)

    theirs = stu.at[pl.ds((1 - core) * sn, sn)]
    remote(theirs, theirs, ssend.at[0], srecv.at[0], sibling).wait_recv()
    low = lax.broadcasted_iota(jnp.int32, (mid, 128), 1) < 64

    def unpack(r):
        base = pl.multiple_of(r * rows, mid)
        for x in range(tn // 2):
            one = stu[r * tn + 2 * x].astype(F32)
            two = stu[r * tn + 2 * x + 1].astype(F32)
            cols = pl.ds(x * 128, 128)
            img_s[pl.ds(base, mid), cols] = jnp.where(low, one, pltpu.roll(two, 64, 1)).astype(BF16)
            img_s[pl.ds(pl.multiple_of(base + mid, mid), mid), cols] = jnp.where(
                low, pltpu.roll(one, 64, 1), two
            ).astype(BF16)

    loop(0, 4, unpack)
    far_own = teach(2, xt_ref, block(far + ylo, 0, rows), sibling)
    far_own.wait_recv()
    teach(3, block(other, 0, rows), block(far + 1 - ylo, 0, rows), sibling).wait_recv()

    for c in range(3):
        text_wait(c, 0, half - 2)
        text_copy(c, 0, half - 1).start()
    for c in range(3):
        text_wait(c, 1, half - 2)
    for c in range(3):
        text_wait(c, 0, half - 1)

    def join(i):
        at = pl.ds(pl.multiple_of(i * 2 * pairs, 16), 2 * pairs)
        two = pl.ds(2 * i, 2)
        text_s[at, :] = buf_s[two].astype(F32).reshape(2 * pairs, ws).astype(BF16)
        text_t[at, pl.ds(0, wh)] = buf_t0[two].astype(F32).reshape(2 * pairs, wh).astype(BF16)
        text_t[at, pl.ds(wh, wh)] = buf_t1[two].astype(F32).reshape(2 * pairs, wh).astype(BF16)

    loop(0, zn // 2, join)

    factor_s = ss_ref[0] / jnp.sqrt(jnp.float32(ws))
    factor_t = st_ref[0] / jnp.sqrt(jnp.float32(wt))

    def scores(i):
        at = pl.ds(pl.multiple_of(i * 256, 256), 256)
        sc_s[:, at] = (
            lax.dot_general(text_s[...], img_s[at, :], NT, preferred_element_type=F32) * factor_s
        )
        sc_t[:, at] = (
            lax.dot_general(text_t[...], img_t[at, :], NT, preferred_element_type=F32) * factor_t
        )

    loop(0, images // 256, scores)

    tile = 2 * pairs
    lane = lax.broadcasted_iota(jnp.int32, (tile, 128), 1)

    def fold(x, op):
        out = x[0:8]
        for k in range(1, tile // 8):
            out = op(out, x[8 * k : 8 * k + 8])
        return out

    def first(i, carry):
        at = pl.ds(pl.multiple_of(i * tile, tile), tile)
        s = sc_s[at, :]
        u = sc_t[at, :]
        ps = jnp.max(s, 1, keepdims=True)
        pt = jnp.max(u, 1, keepdims=True)
        es = jnp.exp(s - ps)
        et = jnp.exp(u - pt)
        e_cs[at, :] = es
        e_ct[at, :] = et
        sums = jnp.sum(es, 1, keepdims=True)
        sumt = jnp.sum(et, 1, keepdims=True)
        mean = jnp.sum(et * s, 1, keepdims=True) / sumt
        ls = ps + jnp.log(sums)
        lt = pt + jnp.log(sumt)
        out = jnp.where(lane == 0, ls, lt)
        out = jnp.where(lane == 3, mean, out)
        out = jnp.where(lane == 4, ps, out)
        colstat[at, :] = jnp.where(lane == 5, pt, out)
        return (
            jnp.maximum(carry[0], fold(s, jnp.maximum)),
            jnp.maximum(carry[1], fold(u, jnp.maximum)),
        )

    start = jnp.full((8, images), -jnp.inf, F32)
    peaks = lax.fori_loop(0, zn // 2, first, (start, start))
    cbuf[0] = colstat[...].T[0:4]

    def c_copy(d):
        return remote(cbuf.at[0], cbuf.at[d], csend.at[d], crecv.at[d], ring(z + d))

    loop(1, zn, lambda d: c_copy(d).start())

    row_ps = jnp.max(peaks[0], 0, keepdims=True)
    row_pt = jnp.max(peaks[1], 0, keepdims=True)

    def second(i, carry):
        at = pl.ds(pl.multiple_of(i * tile, tile), tile)
        s = sc_s[at, :]
        es = jnp.exp(s - row_ps)
        et = jnp.exp(sc_t[at, :] - row_pt)
        e_rs[at, :] = es
        e_rt[at, :] = et
        return (
            carry[0] + fold(es, jnp.add),
            carry[1] + fold(et, jnp.add),
            carry[2] + fold(et * s, jnp.add),
        )

    zero = jnp.zeros((8, images), F32)
    row_sums = lax.fori_loop(0, zn // 2, second, (zero, zero, zero))
    rs, rt, rw = [jnp.sum(x, 0, keepdims=True) for x in row_sums]
    shape = (4, images)
    row = lax.broadcasted_iota(jnp.int32, shape, 0)
    rbuf[0] = jnp.where(
        row == 0, row_ps + jnp.log(rs), jnp.where(row == 3, rw / rt, row_pt + jnp.log(rt))
    )

    def r_copy(d):
        device = plane(lax.rem(me + d, pn))
        return remote(rbuf.at[0], rbuf.at[d], rsend.at[d], rrecv.at[d], device)

    loop(1, pn, lambda d: r_copy(d).start())
    loop(1, zn, lambda d: c_copy(d).wait_recv())
    col_s, col_t, col_loss = combine(cbuf, zn, (4, texts))
    row8 = lax.broadcasted_iota(jnp.int32, (8, texts), 0)
    back = jnp.where(row8 == 0, col_s, jnp.where(row8 == 1, col_t, col_loss))
    back = jnp.concatenate([back, jnp.zeros((120, texts), F32)], 0)
    colback[...] = back.T

    loop(1, pn, lambda d: r_copy(d).wait_recv())
    row_s, row_t, row_loss = combine(rbuf, pn, (4, images))
    row_fs = 0.5 * jnp.exp(row_ps - row_s)
    row_ft = 0.5 * jnp.exp(row_pt - row_t)

    def grads(i):
        at = pl.ds(pl.multiple_of(i * tile, tile), tile)
        fs = 0.5 * jnp.exp(colstat[at, 4:5] - colback[at, 0:1])
        ft = 0.5 * jnp.exp(colstat[at, 5:6] - colback[at, 1:2])
        g = e_rs[at, :] * row_fs - e_rt[at, :] * row_ft + e_cs[at, :] * fs - e_ct[at, :] * ft
        g_ref[at, :] = g.astype(BF16)

    loop(0, zn // 2, grads)

    part = jnp.dot(g_ref[...], img_s[...], preferred_element_type=F32)
    q_ref[...] = part.reshape(zn, pairs, ws)
    wg = ws // 2

    def grad_copy(c, way, s):
        return remote(
            rstage.at[c, way, s],
            rland.at[c, way, s],
            gsend.at[c, way, s],
            grecv.at[c, way, s],
            right if way == 0 else left,
        )

    def grad_owner(way, s):
        if way == 0:
            return lax.rem(z + half - s, zn)
        return lax.rem(z + half + 1 + s, zn)

    for c in range(2):
        for way in range(2):
            rstage[c, way, 0] = q_ref[grad_owner(way, 0), :, c * wg : (c + 1) * wg]
            grad_copy(c, way, 0).start()

    def grad_step(s, ways=(0, 1)):
        for c in range(2):
            for way in ways:
                grad_copy(c, way, s - 1).wait_recv()
                rstage[c, way, s] = (
                    q_ref[grad_owner(way, s), :, c * wg : (c + 1) * wg] + rland[c, way, s - 1]
                )
                grad_copy(c, way, s).start()

    gtr_ref[...] = g_ref[...].astype(F32).T.astype(BF16)

    def image_copy(i, e):
        r = lax.rem(rb + i, 4)
        to = lax.rem(t + e, tn)
        k = i * tn + e
        return remote(
            istage.at[i * tn + to],
            iland.at[k],
            isend.at[k],
            irecv.at[k],
            plane(r * tn + to),
        )

    def image_part(i):
        r = lax.rem(rb + i, 4)
        at = pl.ds(pl.multiple_of(r * rows, mid), rows)
        part = jnp.dot(gtr_ref[at, :], text_s[...], preferred_element_type=F32)
        for x in range(tn // 2):
            top = part[:mid, x * 128 : (x + 1) * 128]
            bottom = part[mid:, x * 128 : (x + 1) * 128]
            istage[i * tn + 2 * x] = jnp.where(low, top, pltpu.roll(bottom, 64, 1)).astype(BF16)
            istage[i * tn + 2 * x + 1] = jnp.where(low, pltpu.roll(top, 64, 1), bottom).astype(BF16)

        def send(e):
            @pl.when(i + e > 0)
            def _():
                image_copy(i, e).start()

        loop(0, tn, send)

    def image_and_ring(i):
        image_part(i)
        grad_step(i + 1)

    loop(0, 4, image_and_ring)
    loop(5, half - 1, grad_step)
    grad_step(half - 1, (0,))

    total = istage[t].astype(F32)

    def image_wait(k):
        image_copy(lax.div(k, tn), lax.rem(k, tn)).wait_recv()

    loop(1, pn, image_wait)
    total = lax.fori_loop(1, pn, lambda k, x: x + iland[k].astype(F32), total) * factor_s
    gi_ref[0:mid, :] = total[:, 0:64]
    gi_ref[mid:rows, :] = total[:, 64:128]

    row16 = lax.broadcasted_iota(jnp.int32, (128, images), 0)
    rowback[...] = jnp.where(row16 == 0, row_loss, 0.0).T
    at_row = pl.ds(pl.multiple_of(rb * rows + t * pairs, 8), pairs)
    at_col = pl.ds(pl.multiple_of(z * pairs, 8), pairs)
    loss_ref[...] = 0.5 * (rowback[at_row, 0:1] + colback[at_col, 2:3])

    for c in range(2):
        grad_copy(c, 1, half - 2).wait_recv()
        grad_copy(c, 0, half - 1).wait_recv()
        cols = slice(c * wg, (c + 1) * wg)
        gt_ref[:, cols] = (
            q_ref[z, :, cols] + rland[c, 0, half - 1] + rland[c, 1, half - 2]
        ) * factor_s

    def sent(s):
        for c in range(3):
            for way in range(2):
                text_copy(c, way, s).wait_send()
        for c in range(2):
            for way in range(2):
                grad_copy(c, way, s).wait_send()

    loop(0, half - 1, sent)
    for c in range(3):
        text_copy(c, 0, half - 1).wait_send()
    for c in range(2):
        grad_copy(c, 0, half - 1).wait_send()
    to_up.wait_send()
    to_down.wait_send()
    to_sib.wait_send()
    to_sib2.wait_send()
    stu_sib.wait_send()
    loop(1, sn, lambda d: stu_copy(d).wait_send())
    loop(1, zn, lambda d: c_copy(d).wait_send())

    def sent_plane(d):
        r_copy(d).wait_send()
        image_copy(lax.div(d, tn), lax.rem(d, tn)).wait_send()

    loop(1, pn, sent_plane)


def body(zn, tn, image_student, text_student, image_teacher, text_teacher, ss, st):
    rows = image_teacher.shape[0]
    pairs, ws = text_student.shape
    wt = text_teacher.shape[1]
    texts, images, mid, half = zn * pairs, 4 * rows, rows // 2, zn // 2
    pn, sn = 4 * tn, 2 * tn
    dma = pltpu.SemaphoreType.DMA
    vmem = pl.BlockSpec(memory_space=pltpu.VMEM)
    smem = pl.BlockSpec(memory_space=pltpu.SMEM)
    score = pltpu.VMEM((texts, images), F32)
    loss, grad_image, grad_text = pl.pallas_call(
        functools.partial(kernel, zn, tn),
        out_shape=(
            jax.ShapeDtypeStruct((pairs, 1), F32),
            jax.ShapeDtypeStruct((rows, ws // tn), F32),
            jax.ShapeDtypeStruct((pairs, ws), F32),
        ),
        in_specs=[vmem, vmem, vmem, vmem, smem, smem],
        out_specs=(vmem, vmem, vmem),
        scratch_shapes=[
            pltpu.VMEM((zn, pairs, ws), BF16),
            pltpu.VMEM((zn, pairs, wt // 2), BF16),
            pltpu.VMEM((zn, pairs, wt // 2), BF16),
            pltpu.VMEM((texts, ws), BF16),
            pltpu.VMEM((texts, wt), BF16),
            pltpu.VMEM((pn, mid, 128), BF16),
            pltpu.VMEM((images, ws), BF16),
            pltpu.VMEM((images, wt), BF16),
            score,
            score,
            score,
            score,
            score,
            score,
            pltpu.VMEM((texts, 128), F32),
            pltpu.VMEM((zn, 4, texts), F32),
            pltpu.VMEM((pn, 4, images), F32),
            pltpu.VMEM((texts, 128), F32),
            pltpu.VMEM((images, 128), F32),
            pltpu.VMEM((texts, images), BF16),
            pltpu.VMEM((images, texts), BF16),
            pltpu.VMEM((zn, pairs, ws), F32),
            pltpu.VMEM((2, 2, half, pairs, ws // 2), F32),
            pltpu.VMEM((2, 2, half, pairs, ws // 2), F32),
            pltpu.VMEM((pn, mid, 128), BF16),
            pltpu.VMEM((pn, mid, 128), BF16),
            dma((3, 2, half)),
            dma((3, 2, half)),
            dma((4,)),
            dma((4,)),
            dma((sn,)),
            dma((sn,)),
            dma((zn,)),
            dma((zn,)),
            dma((pn,)),
            dma((pn,)),
            dma((pn,)),
            dma((pn,)),
            dma((2, 2, half)),
            dma((2, 2, half)),
        ],
        compiler_params=pltpu.CompilerParams(
            collective_id=0, has_side_effects=True, vmem_limit_bytes=50 * 2**20
        ),
    )(image_student, image_teacher, text_student, text_teacher, ss, st)
    return loss.reshape(pairs), grad_image, grad_text


def solution(mesh):
    zn = mesh.shape["batch"] // 4
    tn = mesh.shape["tensor"]
    return jax.shard_map(
        functools.partial(body, zn, tn),
        mesh=mesh,
        in_specs=(
            P("batch", "tensor"),
            P(("batch", "tensor"), None),
            P("batch", None),
            P(("batch", "tensor"), None),
            P(),
            P(),
        ),
        out_specs=(P(("batch", "tensor")), P("batch", "tensor"), P(("batch", "tensor"), None)),
        check_vma=False,
    )
```

time: 931 us -> 92.3 us (0.10)
  the two profiles are of different devices: /device:TPU:1 before, /device:TPU:32 now
where the time goes in v1:
time: 92.3 us; the launch traced here: 92 us
  Pallas kernels  85.4 us (93%)
  local copies, waits for them, and re-layouts  3.96 us (4%)
  between operations  1.96 us (2%)
    pallas_call x1, Pallas kernels, body(): pl.pallas_call(functools.partial(kernel, zn, tn), out_shape=(jax.ShapeDty...  85.4 us
    unnamed x9, local copies, waits for them, and re-layouts  3.96 us

profile of v1, /device:TPU:32, one launch (start us, length us, event | category | flops | bytes accessed | tf_op | source)
XLA Modules:
  0.0 92.0 jit_solution(3783103850340173674)
XLA Ops:
  0.6 0.0 copy-start.1
  1.9 0.9 copy.11.xs_ref
  2.8 0.0 copy-done.1
  2.8 0.0 copy-start
  2.8 1.0 %copy-done = bf16[192,1280]{1,0:T(8,128)(2,1)S(1)} copy-done((bf16[192,1280]{1,0:T(8,128)(2,1)S(1)}, bf16[192,1280]{1,0:T(8,128)(2,1)}, u32[]{:S(2)}) %copy-start) | copy-done | bytes 491544
  3.9 0.0 copy-start.2
  3.9 0.7 copy-done.2
  4.6 85.4 %shard_map.85 = (f32[24,1]{1,0:T(8,128)S(1)}, f32[192,64]{1,0:T(8,128)S(1)}, f32[24,512]{1,0:T(8,128)S(1)}) custom-call(bf16[192,64]{1,0:T(8,128)(2,1)S(1)} %copy.11.xs_ref, bf16[192,1280]{1,0:T(8,128)(2,1)S(1)} %copy-done, bf16[24,512]{1,0:T(8,128)(2,1)S(1)} %copy-done.2, bf16[24,1280]{1,0:T(8,128)(2,1)S(1)} %copy-done.1, f32[1]{0:T(128)S(6)} %copy.14.ss_ref, ...), custom_call_target="tpu_custom_call" | custom-call | tf_op jit(solution)/shard_map/pallas_call | solution.py:511
  90.0 0.6 reduce
  90.6 0.7 copy.12
  91.4 0.6 copy.16
Async XLA Ops:
  0.6 2.2 %copy-start.1 = (bf16[24,1280]{1,0:T(8,128)(2,1)S(1)}, bf16[24,1280]{1,0:T(8,128)(2,1)}, u32[]{:S(2)}) copy-start(bf16[24,1280]{1,0:T(8,128)(2,1)} %tt_ref.1) | copy-start | bytes 184324
  2.8 1.0 %copy-start = (bf16[192,1280]{1,0:T(8,128)(2,1)S(1)}, bf16[192,1280]{1,0:T(8,128)(2,1)}, u32[]{:S(2)}) copy-start(bf16[192,1280]{1,0:T(8,128)(2,1)} %xt_ref.1) | copy-start | bytes 1474564
  3.9 0.7 copy-start.2

commit v2 on v0

v2 whole, which is shorter than its diff:
```python
import functools

import jax
import jax.numpy as jnp
from jax import lax
from jax.experimental import pallas as pl
from jax.experimental.pallas import tpu as pltpu
from jax.sharding import PartitionSpec as P

MESH = pl.DeviceIdType.MESH
F32 = jnp.float32
BF16 = jnp.bfloat16
NN = (((1,), (0,)), ((), ()))
NT = (((1,), (1,)), ((), ()))
SELF = 20


def remote(src, dst, send, recv, device):
    return pltpu.make_async_remote_copy(
        src_ref=src,
        dst_ref=dst,
        send_sem=send,
        recv_sem=recv,
        device_id=device,
        device_id_type=MESH,
    )


def loop(low, high, body):
    def step(i, carry):
        body(i)
        return carry

    lax.fori_loop(low, high, step, 0)


def join_lse(buf, count):
    peak = buf[0]
    for k in range(1, count):
        peak = jnp.maximum(peak, buf[k])
    total = jnp.zeros(peak.shape, F32)
    for k in range(count):
        total = total + jnp.exp(buf[k] - peak)
    return peak + jnp.log(total)


def join_mean(buf, means, lse, count):
    total = jnp.zeros(means[0].shape, F32)
    for k in range(count):
        total = total + jnp.exp(buf[k][1:2] - lse[1:2]) * means[k]
    return total


def kernel(
    zn,
    tn,
    xs_ref,
    xt_ref,
    ts_ref,
    tt_ref,
    ss_ref,
    st_ref,
    loss_ref,
    gi_ref,
    gt_ref,
    xs_v,
    buf_s,
    buf_t0,
    buf_t1,
    text_s,
    text_t,
    text_tr,
    stu,
    img_s,
    img_t,
    sc_s,
    sc_t,
    e_rs,
    e_rt,
    e_cs,
    e_ct,
    colstat,
    cbuf,
    cmean,
    rbuf,
    rmean,
    colback,
    g_ref,
    q_ref,
    p_ref,
    dstage,
    dland,
    hstage,
    hland,
    fstage,
    fland,
    istage,
    iland,
    lsem,
    tsend,
    trecv,
    xsend,
    xrecv,
    ssend,
    srecv,
    csend,
    crecv,
    rsend,
    rrecv,
    isend,
    irecv,
    dsend,
    drecv,
    hsend,
    hrecv,
    fsend,
    frecv,
    cmsend,
    cmrecv,
    rmsend,
    rmrecv,
):
    pn = 4 * tn
    xn = tn // 2
    half = zn // 2
    b = lax.axis_index("batch")
    t = lax.axis_index("tensor")
    z = lax.div(b, 4)
    ylo = lax.rem(lax.div(b, 2), 2)
    core = lax.rem(b, 2)
    x = lax.div(t, 2)
    yhi = lax.rem(t, 2)
    y = yhi * 2 + ylo
    rb = core * 2 + ylo
    rows = xt_ref.shape[0]
    mid = rows // 2
    pairs, ws = ts_ref.shape
    wt = tt_ref.shape[1]
    wh = wt // 2
    wx = ws // tn
    texts = zn * pairs
    images = 4 * rows
    tile = 2 * pairs

    def at_chip(dx, dy, c):
        x2 = lax.rem(x + dx, xn)
        y2 = lax.rem(y + dy, 4)
        return (4 * z + lax.rem(y2, 2) * 2 + c, x2 * 2 + lax.div(y2, 2))

    def ring(d):
        return (lax.rem(z + d, zn) * 4 + ylo * 2 + core, t)

    sibling = (b + 1 - 2 * core, t)
    right = ring(1)
    left = ring(zn - 1)
    near = [right, left, sibling]
    near += [at_chip(d, 0, core) for d in range(1, xn)]
    near += [at_chip(0, d, core) for d in range(1, 4)]
    barrier = pltpu.get_barrier_semaphore()
    for device in near:
        pl.semaphore_signal(barrier, inc=1, device_id=device, device_id_type=MESH)

    bufs = (buf_s, buf_t0, buf_t1)
    own_text = (ts_ref, tt_ref.at[:, pl.ds(0, wh)], tt_ref.at[:, pl.ds(wh, wh)])
    own_xs = pltpu.make_async_copy(xs_ref, xs_v, lsem.at[0])
    own_xs.start()
    local = [pltpu.make_async_copy(own_text[c], bufs[c].at[z], lsem.at[c + 1]) for c in range(3)]

    def block(r, start, size):
        return img_t.at[pl.ds(pl.multiple_of(r * rows + start, mid), size)]

    local.append(pltpu.make_async_copy(xt_ref, block(rb, 0, rows), lsem.at[4]))
    for copy in local:
        copy.start()

    own_xs.wait()
    whole = xs_v[...].astype(F32)
    odd = ylo == 1
    main = jnp.where(odd, whole[:, rows - 128 :], whole[:, :128])
    rest = jnp.where(odd, whole[:, : rows - 128], whole[:, 128:])
    packed = jnp.concatenate([rest[: wx // 2], rest[wx // 2 :]], 1)

    def group(c, y0, y1):
        return ((c * 2 + y0) * 2 + y1) * xn

    own_stu = stu.at[group(core, ylo, yhi) + x]
    own_stu[0:wx, :] = main.astype(BF16)
    own_stu[wx:, :] = packed.astype(BF16)

    pl.semaphore_wait(barrier, len(near))

    def text_copy(c, way, s):
        o = lax.rem(z + (zn - s if way == 0 else s), zn)
        src = own_text[c] if s == 0 else bufs[c].at[o]
        return remote(
            src,
            bufs[c].at[o],
            tsend.at[c, way, s],
            trecv.at[c, way, s],
            right if way == 0 else left,
        )

    def text_wait(c, way, s):
        o = lax.rem(z + (zn - 1 - s if way == 0 else 1 + s), zn)
        slot = bufs[c].at[o]
        remote(
            slot, slot, tsend.at[c, way, s], trecv.at[c, way, s], right if way == 0 else left
        ).wait_recv()

    def text_step(s):
        for c in range(3):
            for way in range(2):
                if s > half - 1 or (way == 1 and s > half - 2):
                    text_wait(c, way, s - 1)
                else:
                    text_wait(c, way, s - 1)
                    text_copy(c, way, s).start()

    for c in range(3):
        for way in range(2):
            text_copy(c, way, 0).start()

    def stu_x(d):
        return remote(own_stu, own_stu, ssend.at[d], srecv.at[d], at_chip(d, 0, core))

    for d in (2, 1, 3):
        stu_x(d).start()

    up = at_chip(0, 1, core)
    down = at_chip(0, 3, core)
    other = core * 2 + 1 - ylo
    far = (1 - core) * 2

    def teach(k, src, dst, device):
        return remote(src, dst, xsend.at[k], xrecv.at[k], device)

    to_up = teach(0, xt_ref.at[pl.ds(0, mid)], block(rb, 0, mid), up)
    to_down = teach(1, xt_ref.at[pl.ds(mid, mid)], block(rb, mid, mid), down)
    to_sib = teach(2, xt_ref, block(rb, 0, rows), sibling)
    to_up.start()
    to_down.start()
    to_sib.start()

    text_step(1)
    for d in range(1, xn):
        slot = stu.at[group(core, ylo, yhi) + lax.rem(x + xn - d, xn)]
        remote(slot, slot, ssend.at[d], srecv.at[d], sibling).wait_recv()

    own_four = stu.at[pl.ds(group(core, ylo, yhi), xn)]

    def stu_y(d):
        return remote(own_four, own_four, ssend.at[3 + d], srecv.at[3 + d], at_chip(0, d, core))

    for d in (2, 1, 3):
        stu_y(d).start()
    text_step(2)
    text_step(3)
    for d in range(1, 4):
        y2 = lax.rem(y + 4 - d, 4)
        slot = stu.at[pl.ds(group(core, lax.rem(y2, 2), lax.div(y2, 2)), xn)]
        remote(slot, slot, ssend.at[3 + d], srecv.at[3 + d], sibling).wait_recv()
    sn = 4 * xn
    mine = stu.at[pl.ds(core * sn, sn)]
    stu_sib = remote(mine, mine, ssend.at[0], srecv.at[0], sibling)
    stu_sib.start()
    teach(0, xt_ref.at[pl.ds(0, mid)], block(other, 0, mid), up).wait_recv()
    teach(1, xt_ref.at[pl.ds(mid, mid)], block(other, mid, mid), down).wait_recv()
    to_sib2 = teach(3, block(other, 0, rows), block(other, 0, rows), sibling)
    to_sib2.start()
    text_step(4)
    for copy in local:
        copy.wait()
    text_step(5)

    theirs = stu.at[pl.ds((1 - core) * sn, sn)]
    remote(theirs, theirs, ssend.at[0], srecv.at[0], sibling).wait_recv()
    low = lax.broadcasted_iota(jnp.int32, (wx // 2, 128), 1) < 64

    def unpack(k):
        c = lax.div(k, tn)
        t2 = lax.rem(k, tn)
        even = stu[group(c, 0, lax.rem(t2, 2)) + lax.div(t2, 2)].astype(F32)
        odds = stu[group(c, 1, lax.rem(t2, 2)) + lax.div(t2, 2)].astype(F32)
        e2 = even[wx:]
        o2 = odds[wx:]
        middle = jnp.concatenate(
            [jnp.where(low, e2, pltpu.roll(o2, 64, 1)), jnp.where(low, pltpu.roll(e2, 64, 1), o2)],
            0,
        )
        at = pl.ds(pl.multiple_of(t2 * wx, wx), wx)
        for k2, part in enumerate((even[:wx], middle, odds[:wx])):
            lanes = pl.ds(pl.multiple_of(c * 2 * rows + k2 * 128, 128), 128)
            img_s[at, lanes] = part.astype(BF16)

    loop(0, 2 * tn, unpack)
    teach(2, xt_ref, block(far + ylo, 0, rows), sibling).wait_recv()
    teach(3, block(other, 0, rows), block(far + 1 - ylo, 0, rows), sibling).wait_recv()

    factor_s = ss_ref[0] / jnp.sqrt(jnp.float32(ws))
    factor_t = st_ref[0] / jnp.sqrt(jnp.float32(wt))
    lane = lax.broadcasted_iota(jnp.int32, (tile, 128), 1)

    def owners(i, last):
        return lax.rem(z + zn - 1 - i, zn), (z if last else lax.rem(z + 1 + i, zn))

    def at_owner(o):
        return pl.ds(pl.multiple_of(o * pairs, 8), pairs)

    def fold(v, op):
        out = v[0:8]
        for k in range(1, tile // 8):
            out = op(out, v[8 * k : 8 * k + 8])
        return out

    def batch(first, end):
        last = end == half

        def at_tile(i):
            return pl.ds(pl.multiple_of(i * tile, tile), tile)

        def join(i):
            o1, o2 = owners(i, last)
            both = lambda buf: jnp.concatenate([buf[o1].astype(F32), buf[o2].astype(F32)], 0)
            text_s[at_tile(i), :] = both(buf_s).astype(BF16)
            text_t[at_tile(i), pl.ds(0, wh)] = both(buf_t0).astype(BF16)
            text_t[at_tile(i), pl.ds(wh, wh)] = both(buf_t1).astype(BF16)

        loop(first, end, join)
        part = pl.ds(first * tile, (end - first) * tile)
        sc_s[part, :] = (
            lax.dot_general(text_s[part, :], img_s[...], NN, preferred_element_type=F32) * factor_s
        )
        sc_t[part, :] = (
            lax.dot_general(text_t[part, :], img_t[...], NT, preferred_element_type=F32) * factor_t
        )

        def columns(i, carry):
            at = at_tile(i)
            s = sc_s[at, :]
            u = sc_t[at, :]
            ps = jnp.max(s, 1, keepdims=True)
            pt = jnp.max(u, 1, keepdims=True)
            es = jnp.exp(s - ps)
            et = jnp.exp(u - pt)
            e_cs[at, :] = es
            e_ct[at, :] = et
            sums = jnp.sum(es, 1, keepdims=True)
            sumt = jnp.sum(et, 1, keepdims=True)
            mean = jnp.sum(et * s, 1, keepdims=True) / sumt
            out = jnp.where(lane == 0, ps + jnp.log(sums), pt + jnp.log(sumt))
            out = jnp.where(lane == 2, mean, out)
            out = jnp.where(lane == 4, ps, out)
            out = jnp.where(lane == 5, pt, out)
            o1, o2 = owners(i, last)
            colstat[at_owner(o1), :] = out[:pairs]
            colstat[at_owner(o2), :] = out[pairs:]
            return (
                jnp.maximum(carry[0], fold(s, jnp.maximum)),
                jnp.maximum(carry[1], fold(u, jnp.maximum)),
            )

        none = jnp.full((8, images), -jnp.inf, F32)
        peaks = lax.fori_loop(first, end, columns, (none, none))
        row_ps = jnp.max(peaks[0], 0, keepdims=True)
        row_pt = jnp.max(peaks[1], 0, keepdims=True)

        def by_rows(i, carry):
            at = at_tile(i)
            s = sc_s[at, :]
            es = jnp.exp(s - row_ps)
            et = jnp.exp(sc_t[at, :] - row_pt)
            e_rs[at, :] = es
            e_rt[at, :] = et
            return (
                carry[0] + fold(es, jnp.add),
                carry[1] + fold(et, jnp.add),
                carry[2] + fold(et * s, jnp.add),
            )

        zero = jnp.zeros((8, images), F32)
        sums = lax.fori_loop(first, end, by_rows, (zero, zero, zero))
        return [row_ps, row_pt] + [jnp.sum(v, 0, keepdims=True) for v in sums]

    cuts = [0, 3, 5, 7, 8]
    stats = [batch(0, 3)]
    text_step(6)
    stats.append(batch(3, 5))
    text_step(7)
    stats.append(batch(5, 7))
    for c in range(3):
        text_wait(c, 0, half - 1)
    stats.append(batch(7, 8))

    across = colstat[...].T
    cbuf[zn - 1] = across[0:2]
    cmean[zn - 1] = across[2:3]

    def ring_place(j):
        return half + (1 - 2 * lax.rem(j, 2)) * lax.div(j + 1, 2)

    def c_copy(j):
        return remote(
            cbuf.at[zn - 1], cbuf.at[j], csend.at[j], crecv.at[j], ring(ring_place(j))
        )

    def cm_copy(j):
        return remote(
            cmean.at[zn - 1], cmean.at[j], cmsend.at[j], cmrecv.at[j], ring(ring_place(j))
        )

    loop(0, zn - 1, lambda j: c_copy(j).start())

    def merged(peak, total):
        top = functools.reduce(jnp.maximum, [s[peak] for s in stats])
        scaled = [jnp.exp(s[peak] - top) for s in stats]
        return top, scaled, sum(f * s[total] for f, s in zip(scaled, stats))

    top_s, _, rs = merged(0, 2)
    top_t, scaled, rt = merged(1, 3)
    rw = sum(f * s[4] for f, s in zip(scaled, stats))
    row = lax.broadcasted_iota(jnp.int32, (2, images), 0)
    rbuf[SELF] = jnp.where(row == 0, top_s + jnp.log(rs), top_t + jnp.log(rt))
    rmean[SELF] = rw / rt

    def chip_of(e):
        return lax.rem(e + 2, 4), lax.rem(lax.div(e, 4) + 2, 4)

    def to_plane(f):
        def each(e):
            for dc in range(2):
                if dc == 0:

                    @pl.when(e != SELF // 2)
                    def _():
                        f(e, dc)

                else:
                    f(e, dc)

        loop(0, 4 * xn, each)

    def plane_copy(buf, send, recv):
        def make(e, dc):
            dx, dy = chip_of(e)
            k = 2 * e + dc
            device = at_chip(dx, dy, 1 - core if dc else core)
            return remote(buf.at[SELF], buf.at[k], send.at[k], recv.at[k], device)

        return make

    r_copy = plane_copy(rbuf, rsend, rrecv)
    rm_copy = plane_copy(rmean, rmsend, rmrecv)
    to_plane(lambda e, dc: r_copy(e, dc).start())
    text_tr[...] = text_s[...].astype(F32).T.astype(BF16)

    loop(0, zn - 1, lambda j: c_copy(j).wait_recv())
    col_lse = join_lse(cbuf, zn)
    colback[...] = jnp.concatenate([col_lse, jnp.zeros((126, texts), F32)], 0).T
    to_plane(lambda e, dc: r_copy(e, dc).wait_recv())
    row_lse = join_lse(rbuf, pn)

    for k in range(4):
        row_fs = 0.5 * jnp.exp(stats[k][0] - row_lse[0:1])
        row_ft = 0.5 * jnp.exp(stats[k][1] - row_lse[1:2])

        def grads(i, last=k == 3, row_fs=row_fs, row_ft=row_ft):
            at = pl.ds(pl.multiple_of(i * tile, tile), tile)
            o1, o2 = owners(i, last)
            here = jnp.concatenate([colstat[at_owner(o1), :], colstat[at_owner(o2), :]], 0)
            lse = jnp.concatenate([colback[at_owner(o1), :], colback[at_owner(o2), :]], 0)
            fs = 0.5 * jnp.exp(here[:, 4:5] - lse[:, 0:1])
            ft = 0.5 * jnp.exp(here[:, 5:6] - lse[:, 1:2])
            g = e_rs[at, :] * row_fs - e_rt[at, :] * row_ft + e_cs[at, :] * fs - e_ct[at, :] * ft
            g_ref[at, :] = g.astype(BF16)

        loop(cuts[k], cuts[k + 1], grads)

    part = lax.dot_general(g_ref[...], img_s[...], NT, preferred_element_type=F32)
    q_ref[...] = part.reshape(zn, pairs, ws)

    def place(way, d):
        return 2 * (half - 1) if d == half else 2 * (d - 1) + (1 if way == 0 else 0)

    def hop(way, d):
        return ring(d if way == 0 else zn - d)

    quarter = half // 2
    relays = [(0, quarter)] + [(w, d) for d in range(quarter - 1, 0, -1) for w in range(2)]
    directs = [(w, d) for d in range(quarter - 1, 0, -1) for w in range(2)]

    def h_copy(k):
        return remote(hstage.at[k], hland.at[k], hsend.at[k], hrecv.at[k], hop(*relays[k]))

    def d_copy(k):
        return remote(dstage.at[k], dland.at[k], dsend.at[k], drecv.at[k], hop(*directs[k]))

    def f_copy(way):
        return remote(
            fstage.at[way], fland.at[way], fsend.at[way], frecv.at[way], hop(way, quarter)
        )

    for k, (way, d) in enumerate(relays):
        hstage[k] = q_ref[place(way, d + quarter)].astype(BF16)
        h_copy(k).start()
    for k, (way, d) in enumerate(directs):
        dstage[k] = q_ref[place(way, d)].astype(BF16)
        d_copy(k).start()

    p_ref[...] = jnp.dot(text_tr[...], g_ref[...], preferred_element_type=F32)

    def pack(k):
        c = lax.div(k, tn)
        t2 = lax.rem(k, tn)
        at = pl.ds(pl.multiple_of(t2 * wx, wx), wx)

        def third(j):
            return p_ref[at, pl.ds(pl.multiple_of(c * 2 * rows + j * 128, 128), 128)]

        middle = third(1)
        m1 = middle[: wx // 2]
        m2 = middle[wx // 2 :]
        even = group(c, 0, lax.rem(t2, 2)) + lax.div(t2, 2)
        odds = group(c, 1, lax.rem(t2, 2)) + lax.div(t2, 2)
        istage[even, pl.ds(0, wx), :] = third(0).astype(BF16)
        istage[odds, pl.ds(0, wx), :] = third(2).astype(BF16)
        istage[even, pl.ds(wx, wx // 2), :] = jnp.where(low, m1, pltpu.roll(m2, 64, 1)).astype(BF16)
        istage[odds, pl.ds(wx, wx // 2), :] = jnp.where(low, pltpu.roll(m1, 64, 1), m2).astype(BF16)

    loop(0, 2 * tn, pack)

    def i_copy(e, dc):
        dx, dy = chip_of(e)
        c = 1 - core if dc else core
        y2 = lax.rem(y + dy, 4)
        src = istage.at[group(c, lax.rem(y2, 2), lax.div(y2, 2)) + lax.rem(x + dx, xn)]
        k = 2 * e + dc
        return remote(src, iland.at[k], isend.at[k], irecv.at[k], at_chip(dx, dy, c))

    to_plane(lambda e, dc: i_copy(e, dc).start())

    for k in range(len(relays)):
        h_copy(k).wait_recv()
    for way in range(2):
        total = q_ref[place(way, quarter)]
        for k, (w, d) in enumerate(relays):
            if w == way:
                total = total + hland[k].astype(F32)
        fstage[way] = total.astype(BF16)
        f_copy(way).start()

    loop(0, zn - 1, lambda j: cm_copy(j).start())
    to_plane(lambda e, dc: rm_copy(e, dc).start())

    to_plane(lambda e, dc: i_copy(e, dc).wait_recv())
    total = istage[group(core, ylo, yhi) + x].astype(F32)
    for k in range(pn):
        if k != SELF:
            total = total + iland[k].astype(F32)
    total = total * factor_s
    main = total[:wx]
    rest = jnp.concatenate([total[wx:, :64], total[wx:, 64:]], 0)
    gi_ref[...] = jnp.where(
        odd, jnp.concatenate([rest, main], 1), jnp.concatenate([main, rest], 1)
    )

    total = q_ref[zn - 1]
    for k in range(len(directs)):
        d_copy(k).wait_recv()
        total = total + dland[k].astype(F32)
    for way in range(2):
        f_copy(way).wait_recv()
        total = total + fland[way].astype(F32)
    gt_ref[...] = total * factor_s

    loop(0, zn - 1, lambda j: cm_copy(j).wait_recv())
    to_plane(lambda e, dc: rm_copy(e, dc).wait_recv())
    col_loss = col_lse[0:1] - join_mean(cbuf, cmean, col_lse, zn)
    row_loss = row_lse[0:1] - join_mean(rbuf, rmean, row_lse, pn)
    own_col = pltpu.roll(jnp.broadcast_to(col_loss, (8, texts)), texts - z * pairs, 1)
    own_row = pltpu.roll(
        jnp.broadcast_to(row_loss, (8, images)), images - rb * rows - t * pairs, 1
    )
    loss_ref[...] = 0.5 * (own_col[0:1, 0:pairs] + own_row[0:1, 0:pairs])

    for s in range(half):
        for c in range(3):
            for way in range(2):
                if way == 0 or s < half - 1:
                    text_copy(c, way, s).wait_send()
    for d in range(1, xn):
        stu_x(d).wait_send()
    for d in range(1, 4):
        stu_y(d).wait_send()
    for copy in (to_up, to_down, to_sib, to_sib2, stu_sib):
        copy.wait_send()
    for k in range(len(relays)):
        h_copy(k).wait_send()
    for k in range(len(directs)):
        d_copy(k).wait_send()
    for way in range(2):
        f_copy(way).wait_send()

    def sent(j):
        c_copy(j).wait_send()
        cm_copy(j).wait_send()

    loop(0, zn - 1, sent)

    def sent_plane(e, dc):
        r_copy(e, dc).wait_send()
        rm_copy(e, dc).wait_send()
        i_copy(e, dc).wait_send()

    to_plane(sent_plane)


def body(zn, tn, image_student, text_student, image_teacher, text_teacher, ss, st):
    rows = image_teacher.shape[0]
    pairs, ws = text_student.shape
    wt = text_teacher.shape[1]
    wx = ws // tn
    texts, images, half = zn * pairs, 4 * rows, zn // 2
    pn = 4 * tn
    high = wx * rows // 128
    dma = pltpu.SemaphoreType.DMA
    anywhere = pl.BlockSpec(memory_space=pl.ANY)
    vmem = pl.BlockSpec(memory_space=pltpu.VMEM)
    smem = pl.BlockSpec(memory_space=pltpu.SMEM)
    score = pltpu.VMEM((texts, images), F32)
    loss, grad_image, grad_text = pl.pallas_call(
        functools.partial(kernel, zn, tn),
        out_shape=(
            jax.ShapeDtypeStruct((1, pairs), F32),
            jax.ShapeDtypeStruct((wx, rows), F32),
            jax.ShapeDtypeStruct((pairs, ws), F32),
        ),
        in_specs=[anywhere] * 4 + [smem, smem],
        out_specs=(vmem, vmem, vmem),
        scratch_shapes=[
            pltpu.VMEM((wx, rows), BF16),
            pltpu.VMEM((zn, pairs, ws), BF16),
            pltpu.VMEM((zn, pairs, wt // 2), BF16),
            pltpu.VMEM((zn, pairs, wt // 2), BF16),
            pltpu.VMEM((texts, ws), BF16),
            pltpu.VMEM((texts, wt), BF16),
            pltpu.VMEM((ws, texts), BF16),
            pltpu.VMEM((pn, high, 128), BF16),
            pltpu.VMEM((ws, images), BF16),
            pltpu.VMEM((images, wt), BF16),
            score,
            score,
            score,
            score,
            score,
            score,
            pltpu.VMEM((texts, 128), F32),
            pltpu.VMEM((zn, 2, texts), F32),
            pltpu.VMEM((zn, 1, texts), F32),
            pltpu.VMEM((pn, 2, images), F32),
            pltpu.VMEM((pn, 1, images), F32),
            pltpu.VMEM((texts, 128), F32),
            pltpu.VMEM((texts, images), BF16),
            pltpu.VMEM((zn, pairs, ws), F32),
            pltpu.VMEM((ws, images), F32),
            pltpu.VMEM((half - 2, pairs, ws), BF16),
            pltpu.VMEM((half - 2, pairs, ws), BF16),
            pltpu.VMEM((half - 1, pairs, ws), BF16),
            pltpu.VMEM((half - 1, pairs, ws), BF16),
            pltpu.VMEM((2, pairs, ws), BF16),
            pltpu.VMEM((2, pairs, ws), BF16),
            pltpu.VMEM((pn, high, 128), BF16),
            pltpu.VMEM((pn, high, 128), BF16),
            dma((5,)),
            dma((3, 2, half)),
            dma((3, 2, half)),
            dma((4,)),
            dma((4,)),
            dma((8,)),
            dma((8,)),
            dma((zn,)),
            dma((zn,)),
            dma((pn,)),
            dma((pn,)),
            dma((pn,)),
            dma((pn,)),
            dma((half - 2,)),
            dma((half - 2,)),
            dma((half - 1,)),
            dma((half - 1,)),
            dma((2,)),
            dma((2,)),
            dma((zn,)),
            dma((zn,)),
            dma((pn,)),
            dma((pn,)),
        ],
        compiler_params=pltpu.CompilerParams(
            collective_id=0, has_side_effects=True, vmem_limit_bytes=62 * 2**20
        ),
    )(image_student.T, image_teacher, text_student, text_teacher, ss, st)
    return loss.reshape(pairs), grad_image.T, grad_text


def solution(mesh):
    zn = mesh.shape["batch"] // 4
    tn = mesh.shape["tensor"]
    return jax.shard_map(
        functools.partial(body, zn, tn),
        mesh=mesh,
        in_specs=(
            P("batch", "tensor"),
            P(("batch", "tensor"), None),
            P("batch", None),
            P(("batch", "tensor"), None),
            P(),
            P(),
        ),
        out_specs=(P(("batch", "tensor")), P("batch", "tensor"), P(("batch", "tensor"), None)),
        check_vma=False,
    )
```

time: 931 us -> 78.6 us (0.08)
  blocking collectives: 483 us -> 0 us
  waiting for transfers between devices: 414 us -> 0 us
  Pallas kernels: 0 us -> 73.2 us
  between operations: 15.2 us -> 1.94 us
  matrix products: 11.1 us -> 0 us
    reduce_scatter x2 -> x0, waiting for transfers between devices: 311 us -> none  [the longest x1 231 us: body(): lax.psum_scatter(lax.dot_general(grads, image_rows, transpose_contract, p...]
    pmax x2 -> x0, blocking collectives: 231 us -> none  [the longest x1 210 us: body(): col_peak = lax.pmax(col_local[0], 'batch')]
    psum x2 -> x0, blocking collectives: 223 us -> none  [the longest x1 207 us: body(): lax.psum((col_local[1] * col_factor, col_local[2] * col_factor[1]), 'batch')]
    all_gather x1 -> x0, waiting for transfers between devices: 102 us -> none  [body(): gathered = lax.all_gather(texts, 'batch', axis=0, tiled=True)]
    pallas_call x0 -> x1, Pallas kernels: none -> 73.2 us  [body(): pl.pallas_call(functools.partial(kernel, zn, tn), out_shape=(jax.ShapeDty...]
    all_gather x1 -> x0, blocking collectives: 29.7 us -> none  [body(): image_rows = lax.all_gather(image_student, 'tensor', axis=1, tiled=True)]
    dot_general x4 -> x0, matrix products: 11.1 us -> none  [the longest x1 3.63 us: local_scores(): lax.dot_general(teacher_rows, piece[:, width:], contract, preferred_eleme...]
  transfers between devices with their start and end apart: 3 -> 0, of which waited for: 3 -> 0; matrix products, arithmetic and copies ran while one was open for 0% -> 0% of each run, Pallas kernels for 0% -> 0%
where the time goes in v2:
time: 78.6 us; the launch traced here: 78.4 us
  Pallas kernels  73.2 us (93%)
  local copies, waits for them, and re-layouts  3.26 us (4%)
  between operations  1.94 us (2%)
    pallas_call x1, Pallas kernels, body(): pl.pallas_call(functools.partial(kernel, zn, tn), out_shape=(jax.ShapeDty...  73.2 us
    unnamed x7, local copies, waits for them, and re-layouts  3.26 us

profile of v2, /device:TPU:1, one launch (start us, length us, event | category | flops | bytes accessed | tf_op | source)
XLA Modules:
  0.0 78.4 jit_solution(11111694049479389701)
XLA Ops:
  1.9 73.2 %shard_map.85 = (f32[1,24]{1,0:T(1,128)}, f32[64,192]{1,0:T(8,128)}, f32[24,512]{1,0:T(8,128)}) custom-call(bf16[64,192]{1,0:T(8,128)(2,1)} %bitcast.4, bf16[192,1280]{1,0:T(8,128)(2,1)} %xt_ref.1, bf16[24,512]{1,0:T(8,128)(2,1)} %ts_ref.1, bf16[24,1280]{1,0:T(8,128)(2,1)} %tt_ref.1, f32[1]{0:T(128)S(6)} %copy.12.ss_ref, f32[1]{0:T(128)S(6)} %copy.13.st_ref), custom_call_target="tpu_custom_call" | custom-call | tf_op jit(solution)/shard_map/pallas_call | solution.py:630
  75.1 0.0 copy-start.1
  75.1 0.6 copy-done.1
  75.7 0.5 copy.14
  76.3 0.0 copy-start
  76.3 1.5 %copy.15 = f32[192,64]{0,1:T(8,128)} copy(f32[192,64]{0,1:T(8,128)} %bitcast.3) | data formatting | bytes 98304
  77.7 0.0 copy-done
  77.7 0.6 copy.16
Async XLA Ops:
  75.1 0.7 copy-start.1
  76.3 1.5 %copy-start = (f32[24,512]{1,0:T(8,128)S(1)}, f32[24,512]{1,0:T(8,128)}, u32[]{:S(2)}) copy-start(f32[24,512]{1,0:T(8,128)} %get-tuple-element.14) | copy-start | bytes 147460

commit v3 on v2

v3 whole, which is shorter than its diff:
```python
import functools

import jax
import jax.numpy as jnp
from jax import lax
from jax.experimental import pallas as pl
from jax.experimental.pallas import tpu as pltpu
from jax.sharding import PartitionSpec as P

MESH = pl.DeviceIdType.MESH
F32 = jnp.float32
BF16 = jnp.bfloat16
NN = (((1,), (0,)), ((), ()))
NT = (((1,), (1,)), ((), ()))


def remote(src, dst, send, recv, device):
    return pltpu.make_async_remote_copy(
        src_ref=src,
        dst_ref=dst,
        send_sem=send,
        recv_sem=recv,
        device_id=device,
        device_id_type=MESH,
    )


def loop(low, high, body):
    def step(i, carry):
        body(i)
        return carry

    lax.fori_loop(low, high, step, 0)


def join_lse(parts):
    peak = functools.reduce(jnp.maximum, parts)
    return peak + jnp.log(sum(jnp.exp(v - peak) for v in parts))


def join_mean(lses, means, lse):
    return sum(jnp.exp(v - lse) * m for v, m in zip(lses, means))


def kernel(
    zn,
    tn,
    xs_ref,
    xt_ref,
    ts_ref,
    tt_ref,
    ss_ref,
    st_ref,
    loss_ref,
    gi_ref,
    gt_ref,
    xs_v,
    buf_a,
    buf_b,
    text_s,
    text_t,
    text_tr,
    stu,
    img_s,
    img_t,
    sc_s,
    sc_t,
    e_rs,
    e_rt,
    e_cs,
    e_ct,
    colstat,
    cbuf,
    cmean,
    rbuf,
    colback,
    g_ref,
    q_ref,
    p_ref,
    dstage,
    dland,
    hstage,
    hland,
    fstage,
    fland,
    sstage,
    sland,
    istage,
    iland,
    rsib,
    lsem,
    tsend,
    trecv,
    xsend,
    xrecv,
    ssend,
    srecv,
    send,
    recv,
):
    xn = tn // 2
    half = zn // 2
    b = lax.axis_index("batch")
    t = lax.axis_index("tensor")
    z = lax.div(b, 4)
    ylo = lax.rem(lax.div(b, 2), 2)
    core = lax.rem(b, 2)
    x = lax.div(t, 2)
    yhi = lax.rem(t, 2)
    y = yhi * 2 + ylo
    rb = core * 2 + ylo
    rows = xt_ref.shape[0]
    mid = rows // 2
    pairs, ws = ts_ref.shape
    wt = tt_ref.shape[1]
    wc = (ws + wt) // 2
    wa = wc - ws
    wx = ws // tn
    texts = zn * pairs
    images = 4 * rows
    tile = 2 * pairs

    def at_chip(dx, dy, c):
        x2 = lax.rem(x + dx, xn)
        y2 = lax.rem(y + dy, 4)
        return (4 * z + lax.rem(y2, 2) * 2 + c, x2 * 2 + lax.div(y2, 2))

    def ring(d):
        return (lax.rem(z + d, zn) * 4 + ylo * 2 + core, t)

    sibling = (b + 1 - 2 * core, t)
    right = ring(1)
    left = ring(zn - 1)
    near = [right, left, sibling]
    near += [at_chip(d, 0, core) for d in range(1, xn)]
    near += [at_chip(0, d, core) for d in range(1, 4)]
    barrier = pltpu.get_barrier_semaphore()
    for device in near:
        pl.semaphore_signal(barrier, inc=1, device_id=device, device_id_type=MESH)

    bufs = (buf_a, buf_b)
    texts_in = [
        pltpu.make_async_copy(ts_ref, buf_a.at[z, :, pl.ds(0, ws)], lsem.at[1]),
        pltpu.make_async_copy(
            tt_ref.at[:, pl.ds(0, wa)], buf_a.at[z, :, pl.ds(ws, wa)], lsem.at[2]
        ),
        pltpu.make_async_copy(tt_ref.at[:, pl.ds(wa, wc)], buf_b.at[z], lsem.at[3]),
    ]
    for copy in texts_in:
        copy.start()
    own_xs = pltpu.make_async_copy(xs_ref, xs_v, lsem.at[0])
    own_xs.start()

    def block(r, start, size):
        return img_t.at[pl.ds(pl.multiple_of(r * rows + start, mid), size)]

    own_xt = pltpu.make_async_copy(xt_ref, block(rb, 0, rows), lsem.at[4])
    own_xt.start()

    for copy in texts_in:
        copy.wait()
    pl.semaphore_wait(barrier, len(near))

    def text_copy(c, way, s):
        o = lax.rem(z + (zn - s if way == 0 else s), zn)
        slot = bufs[c].at[o]
        return remote(
            slot, slot, tsend.at[c], trecv.at[c, way, s], right if way == 0 else left
        )

    def text_wait(c, way, s):
        o = lax.rem(z + (zn - 1 - s if way == 0 else 1 + s), zn)
        slot = bufs[c].at[o]
        remote(slot, slot, tsend.at[c], trecv.at[c, way, s], right).wait_recv()

    def text_step(s):
        for c in range(2):
            for way in range(2):
                if s > half - 1 or (way == 1 and s > half - 2):
                    text_wait(c, way, s - 1)
                else:
                    text_wait(c, way, s - 1)
                    text_copy(c, way, s).start()

    for c in range(2):
        for way in range(2):
            text_copy(c, way, 0).start()

    up = at_chip(0, 1, core)
    down = at_chip(0, 3, core)
    other = core * 2 + 1 - ylo
    far = (1 - core) * 2

    def teach(k, src, dst, device):
        return remote(src, dst, xsend.at[k], xrecv.at[k], device)

    to_up = teach(0, xt_ref.at[pl.ds(0, mid)], block(rb, 0, mid), up)
    to_down = teach(0, xt_ref.at[pl.ds(mid, mid)], block(rb, mid, mid), down)
    to_sib = teach(1, xt_ref, block(rb, 0, rows), sibling)
    to_up.start()
    to_down.start()
    to_sib.start()

    own_xs.wait()
    whole = xs_v[...].astype(F32)
    odd = ylo == 1
    main = jnp.where(odd, whole[:, rows - 128 :], whole[:, :128])
    rest = jnp.where(odd, whole[:, : rows - 128], whole[:, 128:])
    packed = jnp.concatenate([rest[: wx // 2], rest[wx // 2 :]], 1)

    def stu_place(c, x2, y0, y1):
        return (c * xn + x2) * 4 + y0 * 2 + y1

    own_stu = stu.at[stu_place(core, x, ylo, yhi)]
    own_stu[0:wx, :] = main.astype(BF16)
    own_stu[wx:, :] = packed.astype(BF16)

    def stu_y(d):
        return remote(own_stu, own_stu, ssend.at[0], srecv.at[0], at_chip(0, d, core))

    for d in (2, 1, 3):
        stu_y(d).start()

    text_step(1)
    def stu_wait(k, count):
        some = stu.at[pl.ds(0, count)]
        remote(some, some, ssend.at[k], srecv.at[k], sibling).wait_recv()

    stu_wait(0, 3)
    own_four = stu.at[pl.ds(stu_place(core, x, 0, 0), 4)]

    def stu_x(d):
        return remote(own_four, own_four, ssend.at[1], srecv.at[1], at_chip(d, 0, core))

    for d in (2, 1, 3):
        stu_x(d).start()
    text_step(2)
    text_step(3)
    sn = 4 * xn
    stu_wait(1, sn - 4)
    mine = stu.at[pl.ds(core * sn, sn)]
    stu_sib = remote(mine, mine, ssend.at[2], srecv.at[2], sibling)
    stu_sib.start()
    teach(0, xt_ref, block(other, 0, rows), up).wait_recv()
    to_sib2 = teach(1, block(other, 0, rows), block(other, 0, rows), sibling)
    to_sib2.start()
    text_step(4)
    own_xt.wait()
    text_step(5)

    stu_wait(2, sn)
    low = lax.broadcasted_iota(jnp.int32, (wx // 2, 128), 1) < 64

    def unpack(k):
        c = lax.div(k, tn)
        t2 = lax.rem(k, tn)
        even = stu[stu_place(c, lax.div(t2, 2), 0, lax.rem(t2, 2))].astype(F32)
        odds = stu[stu_place(c, lax.div(t2, 2), 1, lax.rem(t2, 2))].astype(F32)
        e2 = even[wx:]
        o2 = odds[wx:]
        middle = jnp.concatenate(
            [jnp.where(low, e2, pltpu.roll(o2, 64, 1)), jnp.where(low, pltpu.roll(e2, 64, 1), o2)],
            0,
        )
        at = pl.ds(pl.multiple_of(t2 * wx, wx), wx)
        for k2, part in enumerate((even[:wx], middle, odds[:wx])):
            lanes = pl.ds(pl.multiple_of(c * 2 * rows + k2 * 128, 128), 128)
            img_s[at, lanes] = part.astype(BF16)

    loop(0, 2 * tn, unpack)
    both_far = img_t.at[pl.ds(pl.multiple_of(far * rows, mid), 2 * rows)]
    teach(1, both_far, both_far, sibling).wait_recv()

    factor_s = ss_ref[0] / jnp.sqrt(jnp.float32(ws))
    factor_t = st_ref[0] / jnp.sqrt(jnp.float32(wt))
    lane = lax.broadcasted_iota(jnp.int32, (tile, 128), 1)

    def owners(i, last):
        return lax.rem(z + zn - 1 - i, zn), (z if last else lax.rem(z + 1 + i, zn))

    def at_owner(o):
        return pl.ds(pl.multiple_of(o * pairs, 8), pairs)

    def fold(v, op):
        out = v[0:8]
        for k in range(1, tile // 8):
            out = op(out, v[8 * k : 8 * k + 8])
        return out

    def batch(first, end):
        last = end == half

        def at_tile(i):
            return pl.ds(pl.multiple_of(i * tile, tile), tile)

        def join(i):
            o1, o2 = owners(i, last)
            both = lambda buf: jnp.concatenate([buf[o1].astype(F32), buf[o2].astype(F32)], 0)
            one = both(buf_a).astype(BF16)
            text_s[at_tile(i), :] = one[:, :ws]
            text_t[at_tile(i), pl.ds(0, wa)] = one[:, ws:]
            text_t[at_tile(i), pl.ds(wa, wc)] = both(buf_b).astype(BF16)

        loop(first, end, join)
        part = pl.ds(first * tile, (end - first) * tile)
        sc_s[part, :] = (
            lax.dot_general(text_s[part, :], img_s[...], NN, preferred_element_type=F32) * factor_s
        )
        sc_t[part, :] = (
            lax.dot_general(text_t[part, :], img_t[...], NT, preferred_element_type=F32) * factor_t
        )

        def columns(i, carry):
            at = at_tile(i)
            s = sc_s[at, :]
            u = sc_t[at, :]
            ps = jnp.max(s, 1, keepdims=True)
            pt = jnp.max(u, 1, keepdims=True)
            es = jnp.exp(s - ps)
            et = jnp.exp(u - pt)
            e_cs[at, :] = es
            e_ct[at, :] = et
            sums = jnp.sum(es, 1, keepdims=True)
            sumt = jnp.sum(et, 1, keepdims=True)
            mean = jnp.sum(et * s, 1, keepdims=True) / sumt
            out = jnp.where(lane == 0, ps + jnp.log(sums), pt + jnp.log(sumt))
            out = jnp.where(lane == 2, mean, out)
            out = jnp.where(lane == 4, ps, out)
            out = jnp.where(lane == 5, pt, out)
            o1, o2 = owners(i, last)
            colstat[at_owner(o1), :] = out[:pairs]
            colstat[at_owner(o2), :] = out[pairs:]
            return (
                jnp.maximum(carry[0], fold(s, jnp.maximum)),
                jnp.maximum(carry[1], fold(u, jnp.maximum)),
            )

        none = jnp.full((8, images), -jnp.inf, F32)
        peaks = lax.fori_loop(first, end, columns, (none, none))
        row_ps = jnp.max(peaks[0], 0, keepdims=True)
        row_pt = jnp.max(peaks[1], 0, keepdims=True)

        def by_rows(i, carry):
            at = at_tile(i)
            s = sc_s[at, :]
            es = jnp.exp(s - row_ps)
            et = jnp.exp(sc_t[at, :] - row_pt)
            e_rs[at, :] = es
            e_rt[at, :] = et
            return (
                carry[0] + fold(es, jnp.add),
                carry[1] + fold(et, jnp.add),
                carry[2] + fold(et * s, jnp.add),
            )

        zero = jnp.zeros((8, images), F32)
        sums = lax.fori_loop(first, end, by_rows, (zero, zero, zero))
        return [row_ps, row_pt] + [jnp.sum(v, 0, keepdims=True) for v in sums]

    cuts = [0, 2, 4, 7, 8]
    stats = [batch(0, 2)]
    text_step(6)
    stats.append(batch(2, 4))
    text_step(7)
    stats.append(batch(4, 7))
    for c in range(2):
        text_wait(c, 0, half - 1)
    stats.append(batch(7, 8))

    across = colstat[...].T
    cbuf[zn - 1] = across[0:2]
    cmean[zn - 1] = across[2:3]

    def ring_place(j):
        return half + (1 - 2 * lax.rem(j, 2)) * lax.div(j + 1, 2)

    def c_copy(j):
        return remote(cbuf.at[zn - 1], cbuf.at[j], send.at[0], recv.at[0], ring(ring_place(j)))

    def cm_copy(j):
        return remote(cmean.at[zn - 1], cmean.at[j], send.at[1], recv.at[1], ring(ring_place(j)))

    def whole_of(buf, k, count):
        some = buf.at[pl.ds(0, count)]
        return remote(some, some, send.at[k], recv.at[k], sibling)

    loop(0, zn - 1, lambda j: c_copy(j).start())

    def merged(peak, total):
        top = functools.reduce(jnp.maximum, [s[peak] for s in stats])
        scaled = [jnp.exp(s[peak] - top) for s in stats]
        return top, scaled, sum(f * s[total] for f, s in zip(scaled, stats))

    top_s, _, rs = merged(0, 2)
    top_t, scaled, rt = merged(1, 3)
    rw = sum(f * s[4] for f, s in zip(scaled, stats))
    row = lax.broadcasted_iota(jnp.int32, (4, images), 0)

    def rows_of(ls, lt, mean):
        return jnp.where(row == 0, ls, jnp.where(row == 1, lt, mean))

    rsib[0] = rows_of(top_s + jnp.log(rs), top_t + jnp.log(rt), rw / rt)
    r_sib = remote(rsib.at[0], rsib.at[1], send.at[2], recv.at[2], sibling)
    r_sib.start()
    r_sib.wait_recv()
    chip = [join_lse([rsib[0][k : k + 1], rsib[1][k : k + 1]]) for k in range(2)]
    chip_mean = join_mean(
        [rsib[0][1:2], rsib[1][1:2]], [rsib[0][2:3], rsib[1][2:3]], chip[1]
    )
    rbuf[sn - 1] = rows_of(chip[0], chip[1], chip_mean)

    def chip_at(m):
        e = m + lax.div(m, 10)
        return lax.rem(e + 2, 4), lax.rem(lax.div(e, 4) + 2, 4)

    def r_copy(m):
        dx, dy = chip_at(m)
        return remote(rbuf.at[sn - 1], rbuf.at[m], send.at[3], recv.at[3], at_chip(dx, dy, core))

    loop(0, sn - 1, lambda m: r_copy(m).start())
    loop(0, zn - 1, lambda j: cm_copy(j).start())
    text_tr[...] = text_s[...].astype(F32).T.astype(BF16)

    whole_of(cbuf, 0, zn - 1).wait_recv()
    col_lse = join_lse([cbuf[k] for k in range(zn)])
    colback[...] = jnp.concatenate([col_lse, jnp.zeros((126, texts), F32)], 0).T
    whole_of(rbuf, 3, sn - 1).wait_recv()
    row_lse = join_lse([rbuf[k] for k in range(sn)])

    def grad_tiles(k):
        row_fs = 0.5 * jnp.exp(stats[k][0] - row_lse[0:1])
        row_ft = 0.5 * jnp.exp(stats[k][1] - row_lse[1:2])

        def grads(i, last=k == 3, row_fs=row_fs, row_ft=row_ft):
            at = pl.ds(pl.multiple_of(i * tile, tile), tile)
            o1, o2 = owners(i, last)
            here = jnp.concatenate([colstat[at_owner(o1), :], colstat[at_owner(o2), :]], 0)
            lse = jnp.concatenate([colback[at_owner(o1), :], colback[at_owner(o2), :]], 0)
            fs = 0.5 * jnp.exp(here[:, 4:5] - lse[:, 0:1])
            ft = 0.5 * jnp.exp(here[:, 5:6] - lse[:, 1:2])
            g = e_rs[at, :] * row_fs - e_rt[at, :] * row_ft + e_cs[at, :] * fs - e_ct[at, :] * ft
            g_ref[at, :] = g.astype(BF16)

        loop(cuts[k], cuts[k + 1], grads)

    def text_part(first, end):
        at = pl.ds(first * tile, (end - first) * tile)
        part = lax.dot_general(g_ref[at, :], img_s[...], NT, preferred_element_type=F32)
        q_ref[2 * first : 2 * end] = part.reshape(2 * (end - first), pairs, ws)


    def place(way, d):
        return 2 * (half - 1) if d == half else 2 * (d - 1) + (1 if way == 0 else 0)

    def hop(way, d):
        return ring(d if way == 0 else zn - d)

    quarter = half // 2
    relays = [(0, quarter)] + [(w, d) for d in range(quarter - 1, 0, -1) for w in range(2)]
    directs = [(w, d) for d in range(quarter - 1, 0, -1) for w in range(2)]

    def h_copy(k):
        return remote(hstage.at[k], hland.at[k], send.at[4], recv.at[4], hop(*relays[k]))

    def d_copy(k):
        return remote(dstage.at[k], dland.at[k], send.at[5], recv.at[5], hop(*directs[k]))

    def f_copy(way):
        return remote(
            fstage.at[way], fland.at[way], send.at[6], recv.at[6], hop(way, quarter)
        )

    grad_tiles(2)
    grad_tiles(3)
    text_part(quarter, half)
    for k, (way, d) in enumerate(relays):
        hstage[k] = q_ref[place(way, d + quarter)].astype(BF16)
        h_copy(k).start()
    grad_tiles(0)
    grad_tiles(1)
    text_part(0, quarter)
    for k, (way, d) in enumerate(directs):
        dstage[k] = q_ref[place(way, d)].astype(BF16)
        d_copy(k).start()

    def image_part(c):
        at = pl.ds(pl.multiple_of(c * 2 * rows, 128), 2 * rows)
        p_ref[...] = jnp.dot(text_tr[...], g_ref[:, at], preferred_element_type=F32)

    def pack(out, more, t2):
        at = pl.ds(pl.multiple_of(t2 * wx, wx), wx)
        middle = p_ref[at, 128:256]
        m1 = middle[: wx // 2]
        m2 = middle[wx // 2 :]
        parts = (
            (p_ref[at, 0:128], jnp.where(low, m1, pltpu.roll(m2, 64, 1))),
            (p_ref[at, 256:384], jnp.where(low, pltpu.roll(m1, 64, 1), m2)),
        )
        for y0, (main, rest) in enumerate(parts):
            k = stu_place(0, lax.div(t2, 2), y0, lax.rem(t2, 2))
            if more is not None:
                main = main + more[k, pl.ds(0, wx), :].astype(F32)
                rest = rest + more[k, pl.ds(wx, wx // 2), :].astype(F32)
            out[k, pl.ds(0, wx), :] = main.astype(BF16)
            out[k, pl.ds(wx, wx // 2), :] = rest.astype(BF16)

    image_part(1 - core)
    loop(0, tn, lambda t2: pack(sstage, None, t2))
    i_sib = remote(sstage, sland, send.at[7], recv.at[7], sibling)
    i_sib.start()
    image_part(core)
    i_sib.wait_recv()
    loop(0, tn, lambda t2: pack(istage, sland, t2))

    def i_copy(m):
        dx, dy = chip_at(m)
        y2 = lax.rem(y + dy, 4)
        src = istage.at[
            stu_place(0, lax.rem(x + dx, xn), lax.rem(y2, 2), lax.div(y2, 2))
        ]
        return remote(src, iland.at[m], send.at[8], recv.at[8], at_chip(dx, dy, core))

    loop(0, sn - 1, lambda m: i_copy(m).start())

    whole_of(hland, 4, len(relays)).wait_recv()
    for way in range(2):
        total = q_ref[place(way, quarter)]
        for k, (w, d) in enumerate(relays):
            if w == way:
                total = total + hland[k].astype(F32)
        fstage[way] = total.astype(BF16)
        f_copy(way).start()

    whole_of(cmean, 1, zn - 1).wait_recv()
    col_mean = join_mean(
        [cbuf[k][1:2] for k in range(zn)], [cmean[k] for k in range(zn)], col_lse[1:2]
    )
    row_mean = join_mean(
        [rbuf[k][1:2] for k in range(sn)], [rbuf[k][2:3] for k in range(sn)], row_lse[1:2]
    )
    col_loss = col_lse[0:1] - col_mean
    row_loss = row_lse[0:1] - row_mean
    own_col = pltpu.roll(jnp.broadcast_to(col_loss, (8, texts)), texts - z * pairs, 1)
    own_row = pltpu.roll(
        jnp.broadcast_to(row_loss, (8, images)), images - rb * rows - t * pairs, 1
    )
    loss_ref[...] = 0.5 * (own_col[0:1, 0:pairs] + own_row[0:1, 0:pairs])

    for c in range(2):
        some = bufs[c].at[pl.ds(0, zn - 1)]
        remote(some, some, tsend.at[c], trecv.at[c, 0, 0], sibling).wait_send()
    for k, count in ((0, 3), (1, 12), (2, sn)):
        some = stu.at[pl.ds(0, count)]
        remote(some, some, ssend.at[k], srecv.at[k], sibling).wait_send()
    teach(0, xt_ref, block(rb, 0, rows), sibling).wait_send()
    teach(1, both_far, both_far, sibling).wait_send()
    whole_of(cbuf, 0, zn - 1).wait_send()
    whole_of(cmean, 1, zn - 1).wait_send()
    r_sib.wait_send()
    whole_of(rbuf, 3, sn - 1).wait_send()
    whole_of(hstage, 4, len(relays)).wait_send()
    whole_of(dstage, 5, len(directs)).wait_send()
    i_sib.wait_send()

    whole_of(iland, 8, sn - 1).wait_recv()
    total = istage[stu_place(0, x, ylo, yhi)].astype(F32)
    for k in range(sn - 1):
        total = total + iland[k].astype(F32)
    total = total * factor_s
    main = total[:wx]
    rest = jnp.concatenate([total[wx:, :64], total[wx:, 64:]], 0)
    gi_ref[...] = jnp.where(
        odd, jnp.concatenate([rest, main], 1), jnp.concatenate([main, rest], 1)
    )
    whole_of(iland, 8, sn - 1).wait_send()

    whole_of(dland, 5, len(directs)).wait_recv()
    total = q_ref[zn - 1]
    for k in range(len(directs)):
        total = total + dland[k].astype(F32)
    whole_of(fland, 6, 2).wait_recv()
    for way in range(2):
        total = total + fland[way].astype(F32)
    gt_ref[...] = total * factor_s
    whole_of(fland, 6, 2).wait_send()


def deliver(loss_ref, image_ref, text_ref, loss_out, image_out, text_out):
    loss_out[...] = loss_ref[...]
    image_out[...] = image_ref[...]
    text_out[...] = text_ref[...]


def body(zn, tn, image_student, text_student, image_teacher, text_teacher, ss, st):
    rows = image_teacher.shape[0]
    pairs, ws = text_student.shape
    wt = text_teacher.shape[1]
    wx = ws // tn
    texts, images, half = zn * pairs, 4 * rows, zn // 2
    sn = 2 * tn
    high = wx * rows // 128
    dma = pltpu.SemaphoreType.DMA
    anywhere = pl.BlockSpec(memory_space=pl.ANY)
    vmem = pl.BlockSpec(memory_space=pltpu.VMEM)
    smem = pl.BlockSpec(memory_space=pltpu.SMEM)
    score = pltpu.VMEM((texts, images), F32)
    loss, grad_image, grad_text = pl.pallas_call(
        functools.partial(kernel, zn, tn),
        out_shape=(
            jax.ShapeDtypeStruct((1, pairs), F32),
            jax.ShapeDtypeStruct((wx, rows), F32),
            jax.ShapeDtypeStruct((pairs, ws), F32),
        ),
        in_specs=[anywhere] * 4 + [smem, smem],
        out_specs=(vmem, vmem, vmem),
        scratch_shapes=[
            pltpu.VMEM((wx, rows), BF16),
            pltpu.VMEM((zn, pairs, (ws + wt) // 2), BF16),
            pltpu.VMEM((zn, pairs, (ws + wt) // 2), BF16),
            pltpu.VMEM((texts, ws), BF16),
            pltpu.VMEM((texts, wt), BF16),
            pltpu.VMEM((ws, texts), BF16),
            pltpu.VMEM((2 * sn, high, 128), BF16),
            pltpu.VMEM((ws, images), BF16),
            pltpu.VMEM((images, wt), BF16),
            score,
            score,
            score,
            score,
            score,
            score,
            pltpu.VMEM((texts, 128), F32),
            pltpu.VMEM((zn, 2, texts), F32),
            pltpu.VMEM((zn, 1, texts), F32),
            pltpu.VMEM((sn, 4, images), F32),
            pltpu.VMEM((texts, 128), F32),
            pltpu.VMEM((texts, images), BF16),
            pltpu.VMEM((zn, pairs, ws), F32),
            pltpu.VMEM((ws, 2 * rows), F32),
            pltpu.VMEM((half - 2, pairs, ws), BF16),
            pltpu.VMEM((half - 2, pairs, ws), BF16),
            pltpu.VMEM((half - 1, pairs, ws), BF16),
            pltpu.VMEM((half - 1, pairs, ws), BF16),
            pltpu.VMEM((2, pairs, ws), BF16),
            pltpu.VMEM((2, pairs, ws), BF16),
            pltpu.VMEM((sn, high, 128), BF16),
            pltpu.VMEM((sn, high, 128), BF16),
            pltpu.VMEM((sn, high, 128), BF16),
            pltpu.VMEM((sn - 1, high, 128), BF16),
            pltpu.VMEM((2, 4, images), F32),
            dma((5,)),
            dma((2,)),
            dma((2, 2, half)),
            dma((2,)),
            dma((2,)),
            dma((3,)),
            dma((3,)),
            dma((9,)),
            dma((9,)),
        ],
        compiler_params=pltpu.CompilerParams(
            collective_id=0, has_side_effects=True, vmem_limit_bytes=62 * 2**20
        ),
    )(image_student.T, image_teacher, text_student, text_teacher, ss, st)
    loss, grad_image, grad_text = pl.pallas_call(
        deliver,
        out_shape=[jax.ShapeDtypeStruct(v.shape, F32) for v in (loss, grad_image, grad_text)],
        in_specs=[vmem] * 3,
        out_specs=[vmem] * 3,
    )(loss, grad_image, grad_text)
    return loss.reshape(pairs), grad_image.T, grad_text


def solution(mesh):
    zn = mesh.shape["batch"] // 4
    tn = mesh.shape["tensor"]
    return jax.shard_map(
        functools.partial(body, zn, tn),
        mesh=mesh,
        in_specs=(
            P("batch", "tensor"),
            P(("batch", "tensor"), None),
            P("batch", None),
            P(("batch", "tensor"), None),
            P(),
            P(),
        ),
        out_specs=(P(("batch", "tensor")), P("batch", "tensor"), P(("batch", "tensor"), None)),
        check_vma=False,
    )
```

time: 78.6 us -> 72.4 us (0.921)
  local copies, waits for them, and re-layouts: 3.26 us -> 0 us
  Pallas kernels: 73.2 us -> 70.3 us
    pallas_call x1, Pallas kernels: 73.2 us -> 68.8 us  [body(): pl.pallas_call(functools.partial(kernel, zn, tn), out_shape=(jax.ShapeDty...]
    unnamed x7 -> x0, local copies, waits for them, and re-layouts: 3.26 us -> none
    pallas_call x0 -> x1, Pallas kernels: none -> 1.49 us  [body(): pl.pallas_call(deliver, out_shape=[jax.ShapeDtypeStruct(v.shape, F32) for...]
where the time goes in v3:
time: 72.4 us; the launch traced here: 72.2 us
  Pallas kernels  70.3 us (97%)
  between operations  1.93 us (3%)
    pallas_call x1, Pallas kernels, body(): pl.pallas_call(functools.partial(kernel, zn, tn), out_shape=(jax.ShapeDty...  68.8 us
    pallas_call x1, Pallas kernels, body(): pl.pallas_call(deliver, out_shape=[jax.ShapeDtypeStruct(v.shape, F32) for...  1.49 us

profile of v3, /device:TPU:1, one launch (start us, length us, event | category | flops | bytes accessed | tf_op | source)
XLA Modules:
  0.0 72.2 jit_solution(2502071755268420848)
XLA Ops:
  1.9 68.8 %shard_map.85 = (f32[1,24]{1,0:T(1,128)}, f32[64,192]{1,0:T(8,128)}, f32[24,512]{1,0:T(8,128)}) custom-call(bf16[64,192]{1,0:T(8,128)(2,1)} %bitcast.3, bf16[192,1280]{1,0:T(8,128)(2,1)} %xt_ref.1, bf16[24,512]{1,0:T(8,128)(2,1)} %ts_ref.1, bf16[24,1280]{1,0:T(8,128)(2,1)} %tt_ref.1, f32[1]{0:T(128)S(6)} %copy.9.ss_ref, f32[1]{0:T(128)S(6)} %copy.10.st_ref), custom_call_target="tpu_custom_call" | custom-call | tf_op jit(solution)/shard_map/pallas_call | solution.py:607
  70.7 1.5 %shard_map.86 = (f32[1,24]{1,0:T(1,128)}, f32[64,192]{1,0:T(8,128)}, f32[24,512]{1,0:T(8,128)}) custom-call(f32[1,24]{1,0:T(1,128)} %get-tuple-element.9.loss_ref, f32[64,192]{1,0:T(8,128)} %get-tuple-element.10.image_ref, f32[24,512]{1,0:T(8,128)} %get-tuple-element.11.text_ref), custom_call_target="tpu_custom_call" | custom-call | tf_op jit(solution)/shard_map/pallas_call | solution.py:665

commit v4 on v3

--- a/solution.py
+++ b/solution.py
@@ -73,6 +73,7 @@
     cbuf,
     cmean,
     rbuf,
+    rmean,
     colback,
     g_ref,
     q_ref,
@@ -81,6 +82,8 @@
     dland,
     hstage,
     hland,
+    ostage,
+    oland,
     fstage,
     fland,
     sstage,
@@ -157,6 +160,20 @@
     own_xt = pltpu.make_async_copy(xt_ref, block(rb, 0, rows), lsem.at[4])
     own_xt.start()
 
+    own_xs.wait()
+    whole = xs_v[...].astype(F32)
+    odd = ylo == 1
+    main = jnp.where(odd, whole[:, rows - 128 :], whole[:, :128])
+    rest = jnp.where(odd, whole[:, : rows - 128], whole[:, 128:])
+    packed = jnp.concatenate([rest[: wx // 2], rest[wx // 2 :]], 1)
+
+    def stu_place(c, x2, y0, y1):
+        return (c * xn + x2) * 4 + y0 * 2 + y1
+
+    own_stu = stu.at[stu_place(core, x, ylo, yhi)]
+    own_stu[0:wx, :] = main.astype(BF16)
+    own_stu[wx:, :] = packed.astype(BF16)
+
     for copy in texts_in:
         copy.wait()
     pl.semaphore_wait(barrier, len(near))
@@ -186,6 +203,12 @@
         for way in range(2):
             text_copy(c, way, 0).start()
 
+    def stu_y(d):
+        return remote(own_stu, own_stu, ssend.at[0], srecv.at[0], at_chip(0, d, core))
+
+    for d in (2, 1, 3):
+        stu_y(d).start()
+
     up = at_chip(0, 1, core)
     down = at_chip(0, 3, core)
     other = core * 2 + 1 - ylo
@@ -201,26 +224,6 @@
     to_down.start()
     to_sib.start()
 
-    own_xs.wait()
-    whole = xs_v[...].astype(F32)
-    odd = ylo == 1
-    main = jnp.where(odd, whole[:, rows - 128 :], whole[:, :128])
-    rest = jnp.where(odd, whole[:, : rows - 128], whole[:, 128:])
-    packed = jnp.concatenate([rest[: wx // 2], rest[wx // 2 :]], 1)
-
-    def stu_place(c, x2, y0, y1):
-        return (c * xn + x2) * 4 + y0 * 2 + y1
-
-    own_stu = stu.at[stu_place(core, x, ylo, yhi)]
-    own_stu[0:wx, :] = main.astype(BF16)
-    own_stu[wx:, :] = packed.astype(BF16)
-
-    def stu_y(d):
-        return remote(own_stu, own_stu, ssend.at[0], srecv.at[0], at_chip(0, d, core))
-
-    for d in (2, 1, 3):
-        stu_y(d).start()
-
     text_step(1)
     def stu_wait(k, count):
         some = stu.at[pl.ds(0, count)]
@@ -237,16 +240,15 @@
     text_step(2)
     text_step(3)
     sn = 4 * xn
+    teach(0, xt_ref, block(other, 0, rows), up).wait_recv()
+    to_sib2 = teach(1, block(other, 0, rows), block(other, 0, rows), sibling)
+    to_sib2.start()
     stu_wait(1, sn - 4)
     mine = stu.at[pl.ds(core * sn, sn)]
     stu_sib = remote(mine, mine, ssend.at[2], srecv.at[2], sibling)
     stu_sib.start()
-    teach(0, xt_ref, block(other, 0, rows), up).wait_recv()
-    to_sib2 = teach(1, block(other, 0, rows), block(other, 0, rows), sibling)
-    to_sib2.start()
     text_step(4)
     own_xt.wait()
-    text_step(5)
 
     stu_wait(2, sn)
     low = lax.broadcasted_iota(jnp.int32, (wx // 2, 128), 1) < 64
@@ -275,8 +277,9 @@
     factor_t = st_ref[0] / jnp.sqrt(jnp.float32(wt))
     lane = lax.broadcasted_iota(jnp.int32, (tile, 128), 1)
 
-    def owners(i, last):
-        return lax.rem(z + zn - 1 - i, zn), (z if last else lax.rem(z + 1 + i, zn))
+    def owners(i):
+        more = 1 - lax.div(i, half - 1)
+        return lax.rem(z + zn - 1 - i, zn), lax.rem(z + (1 + i) * more, zn)
 
     def at_owner(o):
         return pl.ds(pl.multiple_of(o * pairs, 8), pairs)
@@ -293,22 +296,40 @@
         def at_tile(i):
             return pl.ds(pl.multiple_of(i * tile, tile), tile)
 
-        def join(i):
-            o1, o2 = owners(i, last)
-            both = lambda buf: jnp.concatenate([buf[o1].astype(F32), buf[o2].astype(F32)], 0)
-            one = both(buf_a).astype(BF16)
+        def both(buf, i):
+            o1, o2 = owners(i)
+            return jnp.concatenate([buf[o1].astype(F32), buf[o2].astype(F32)], 0).astype(BF16)
+
+        def join_a(i):
+            one = both(buf_a, i)
             text_s[at_tile(i), :] = one[:, :ws]
             text_t[at_tile(i), pl.ds(0, wa)] = one[:, ws:]
-            text_t[at_tile(i), pl.ds(wa, wc)] = both(buf_b).astype(BF16)
-
-        loop(first, end, join)
+
+        def join_b(i):
+            text_t[at_tile(i), pl.ds(wa, wc)] = both(buf_b, i)
+
         part = pl.ds(first * tile, (end - first) * tile)
+
+        def teacher(start, size):
+            at = pl.ds(start, size)
+            return lax.dot_general(
+                text_t[part, at], img_t[:, at], NT, preferred_element_type=F32
+            )
+
+        if last:
+            text_wait(0, 0, half - 1)
+        loop(first, end, join_a)
         sc_s[part, :] = (
             lax.dot_general(text_s[part, :], img_s[...], NN, preferred_element_type=F32) * factor_s
         )
-        sc_t[part, :] = (
-            lax.dot_general(text_t[part, :], img_t[...], NT, preferred_element_type=F32) * factor_t
-        )
+        if last:
+            sc_t[part, :] = teacher(0, wa)
+            text_wait(1, 0, half - 1)
+        loop(first, end, join_b)
+        if last:
+            sc_t[part, :] = (sc_t[part, :] + teacher(wa, wc)) * factor_t
+        else:
+            sc_t[part, :] = teacher(0, wt) * factor_t
 
         def columns(i, carry):
             at = at_tile(i)
@@ -327,7 +348,7 @@
             out = jnp.where(lane == 2, mean, out)
             out = jnp.where(lane == 4, ps, out)
             out = jnp.where(lane == 5, pt, out)
-            o1, o2 = owners(i, last)
+            o1, o2 = owners(i)
             colstat[at_owner(o1), :] = out[:pairs]
             colstat[at_owner(o2), :] = out[pairs:]
             return (
@@ -357,20 +378,6 @@
         sums = lax.fori_loop(first, end, by_rows, (zero, zero, zero))
         return [row_ps, row_pt] + [jnp.sum(v, 0, keepdims=True) for v in sums]
 
-    cuts = [0, 2, 4, 7, 8]
-    stats = [batch(0, 2)]
-    text_step(6)
-    stats.append(batch(2, 4))
-    text_step(7)
-    stats.append(batch(4, 7))
-    for c in range(2):
-        text_wait(c, 0, half - 1)
-    stats.append(batch(7, 8))
-
-    across = colstat[...].T
-    cbuf[zn - 1] = across[0:2]
-    cmean[zn - 1] = across[2:3]
-
     def ring_place(j):
         return half + (1 - 2 * lax.rem(j, 2)) * lax.div(j + 1, 2)
 
@@ -384,7 +391,19 @@
         some = buf.at[pl.ds(0, count)]
         return remote(some, some, send.at[k], recv.at[k], sibling)
 
-    loop(0, zn - 1, lambda j: c_copy(j).start())
+    def send_columns():
+        across = colstat[...].T
+        cbuf[zn - 1] = across[0:2]
+        cmean[zn - 1] = across[2:3]
+        loop(0, zn - 1, lambda j: c_copy(j).start())
+
+    cuts = [0, 4, 6, 8]
+    text_step(5)
+    stats = [batch(0, 4)]
+    text_step(6)
+    text_step(7)
+    stats.append(batch(4, 6))
+    stats.append(batch(6, 8))
 
     def merged(peak, total):
         top = functools.reduce(jnp.maximum, [s[peak] for s in stats])
@@ -402,12 +421,14 @@
     rsib[0] = rows_of(top_s + jnp.log(rs), top_t + jnp.log(rt), rw / rt)
     r_sib = remote(rsib.at[0], rsib.at[1], send.at[2], recv.at[2], sibling)
     r_sib.start()
+    send_columns()
     r_sib.wait_recv()
     chip = [join_lse([rsib[0][k : k + 1], rsib[1][k : k + 1]]) for k in range(2)]
     chip_mean = join_mean(
         [rsib[0][1:2], rsib[1][1:2]], [rsib[0][2:3], rsib[1][2:3]], chip[1]
     )
-    rbuf[sn - 1] = rows_of(chip[0], chip[1], chip_mean)
+    rbuf[sn - 1] = rows_of(chip[0], chip[1], chip_mean)[0:2]
+    rmean[sn - 1] = chip_mean
 
     def chip_at(m):
         e = m + lax.div(m, 10)
@@ -417,23 +438,29 @@
         dx, dy = chip_at(m)
         return remote(rbuf.at[sn - 1], rbuf.at[m], send.at[3], recv.at[3], at_chip(dx, dy, core))
 
+    def rm_copy(m):
+        dx, dy = chip_at(m)
+        device = at_chip(dx, dy, core)
+        return remote(rmean.at[sn - 1], rmean.at[m], send.at[10], recv.at[10], device)
+
     loop(0, sn - 1, lambda m: r_copy(m).start())
     loop(0, zn - 1, lambda j: cm_copy(j).start())
+    loop(0, sn - 1, lambda m: rm_copy(m).start())
     text_tr[...] = text_s[...].astype(F32).T.astype(BF16)
 
+    whole_of(rbuf, 3, sn - 1).wait_recv()
+    row_lse = join_lse([rbuf[k] for k in range(sn)])
     whole_of(cbuf, 0, zn - 1).wait_recv()
     col_lse = join_lse([cbuf[k] for k in range(zn)])
     colback[...] = jnp.concatenate([col_lse, jnp.zeros((126, texts), F32)], 0).T
-    whole_of(rbuf, 3, sn - 1).wait_recv()
-    row_lse = join_lse([rbuf[k] for k in range(sn)])
 
     def grad_tiles(k):
         row_fs = 0.5 * jnp.exp(stats[k][0] - row_lse[0:1])
         row_ft = 0.5 * jnp.exp(stats[k][1] - row_lse[1:2])
 
-        def grads(i, last=k == 3, row_fs=row_fs, row_ft=row_ft):
+        def grads(i, row_fs=row_fs, row_ft=row_ft):
             at = pl.ds(pl.multiple_of(i * tile, tile), tile)
-            o1, o2 = owners(i, last)
+            o1, o2 = owners(i)
             here = jnp.concatenate([colstat[at_owner(o1), :], colstat[at_owner(o2), :]], 0)
             lse = jnp.concatenate([colback[at_owner(o1), :], colback[at_owner(o2), :]], 0)
             fs = 0.5 * jnp.exp(here[:, 4:5] - lse[:, 0:1])
@@ -456,28 +483,37 @@
         return ring(d if way == 0 else zn - d)
 
     quarter = half // 2
-    relays = [(0, quarter)] + [(w, d) for d in range(quarter - 1, 0, -1) for w in range(2)]
-    directs = [(w, d) for d in range(quarter - 1, 0, -1) for w in range(2)]
+    relays = [(w, d) for d in range(quarter - 1, 0, -1) for w in range(2)]
+    directs = relays
+    wg = ws // 2
 
     def h_copy(k):
         return remote(hstage.at[k], hland.at[k], send.at[4], recv.at[4], hop(*relays[k]))
 
     def d_copy(k):
         return remote(dstage.at[k], dland.at[k], send.at[5], recv.at[5], hop(*directs[k]))
+
+    def o_copy(way):
+        return remote(
+            ostage.at[way], oland.at[way], send.at[9], recv.at[9], hop(way, quarter)
+        )
 
     def f_copy(way):
         return remote(
             fstage.at[way], fland.at[way], send.at[6], recv.at[6], hop(way, quarter)
         )
 
+    grad_tiles(1)
     grad_tiles(2)
-    grad_tiles(3)
     text_part(quarter, half)
+    for way in range(2):
+        ostage[way] = q_ref[place(way, half), :, way * wg : (way + 1) * wg].astype(BF16)
+        o_copy(way).start()
     for k, (way, d) in enumerate(relays):
         hstage[k] = q_ref[place(way, d + quarter)].astype(BF16)
         h_copy(k).start()
     grad_tiles(0)
-    grad_tiles(1)
+
     text_part(0, quarter)
     for k, (way, d) in enumerate(directs):
         dstage[k] = q_ref[place(way, d)].astype(BF16)
@@ -523,20 +559,25 @@
     loop(0, sn - 1, lambda m: i_copy(m).start())
 
     whole_of(hland, 4, len(relays)).wait_recv()
+    whole_of(oland, 9, 2).wait_recv()
     for way in range(2):
         total = q_ref[place(way, quarter)]
         for k, (w, d) in enumerate(relays):
             if w == way:
                 total = total + hland[k].astype(F32)
+        farthest = oland[way].astype(F32)
+        zero = jnp.zeros((pairs, wg), F32)
+        total = total + jnp.concatenate([farthest, zero] if way == 0 else [zero, farthest], 1)
         fstage[way] = total.astype(BF16)
         f_copy(way).start()
 
     whole_of(cmean, 1, zn - 1).wait_recv()
+    whole_of(rmean, 10, sn - 1).wait_recv()
     col_mean = join_mean(
         [cbuf[k][1:2] for k in range(zn)], [cmean[k] for k in range(zn)], col_lse[1:2]
     )
     row_mean = join_mean(
-        [rbuf[k][1:2] for k in range(sn)], [rbuf[k][2:3] for k in range(sn)], row_lse[1:2]
+        [rbuf[k][1:2] for k in range(sn)], [rmean[k] for k in range(sn)], row_lse[1:2]
     )
     col_loss = col_lse[0:1] - col_mean
     row_loss = row_lse[0:1] - row_mean
@@ -558,7 +599,9 @@
     whole_of(cmean, 1, zn - 1).wait_send()
     r_sib.wait_send()
     whole_of(rbuf, 3, sn - 1).wait_send()
+    whole_of(rmean, 10, sn - 1).wait_send()
     whole_of(hstage, 4, len(relays)).wait_send()
+    whole_of(ostage, 9, 2).wait_send()
     whole_of(dstage, 5, len(directs)).wait_send()
     i_sib.wait_send()
 
@@ -632,15 +675,18 @@
             pltpu.VMEM((texts, 128), F32),
             pltpu.VMEM((zn, 2, texts), F32),
             pltpu.VMEM((zn, 1, texts), F32),
-            pltpu.VMEM((sn, 4, images), F32),
+            pltpu.VMEM((sn, 2, images), F32),
+            pltpu.VMEM((sn, 1, images), F32),
             pltpu.VMEM((texts, 128), F32),
             pltpu.VMEM((texts, images), BF16),
             pltpu.VMEM((zn, pairs, ws), F32),
             pltpu.VMEM((ws, 2 * rows), F32),
             pltpu.VMEM((half - 2, pairs, ws), BF16),
             pltpu.VMEM((half - 2, pairs, ws), BF16),
-            pltpu.VMEM((half - 1, pairs, ws), BF16),
-            pltpu.VMEM((half - 1, pairs, ws), BF16),
+            pltpu.VMEM((half - 2, pairs, ws), BF16),
+            pltpu.VMEM((half - 2, pairs, ws), BF16),
+            pltpu.VMEM((2, pairs, ws // 2), BF16),
+            pltpu.VMEM((2, pairs, ws // 2), BF16),
             pltpu.VMEM((2, pairs, ws), BF16),
             pltpu.VMEM((2, pairs, ws), BF16),
             pltpu.VMEM((sn, high, 128), BF16),
@@ -655,8 +701,8 @@
             dma((2,)),
             dma((3,)),
             dma((3,)),
-            dma((9,)),
-            dma((9,)),
+            dma((11,)),
+            dma((11,)),
         ],
         compiler_params=pltpu.CompilerParams(
             collective_id=0, has_side_effects=True, vmem_limit_bytes=62 * 2**20

time: 72.4 us -> 68.7 us (0.949)
  Pallas kernels: 70.3 us -> 66.6 us
    pallas_call x1, Pallas kernels: 68.8 us -> 65.1 us  [body(): pl.pallas_call(functools.partial(kernel, zn, tn), out_shape=(jax.ShapeDty...]
where the time goes in v4:
time: 68.7 us; the launch traced here: 68.5 us
  Pallas kernels  66.6 us (97%)
  between operations  1.93 us (3%)
    pallas_call x1, Pallas kernels, body(): pl.pallas_call(functools.partial(kernel, zn, tn), out_shape=(jax.ShapeDty...  65.1 us
    pallas_call x1, Pallas kernels, body(): pl.pallas_call(deliver, out_shape=[jax.ShapeDtypeStruct(v.shape, F32) for...  1.49 us

profile of v4, /device:TPU:1, one launch (start us, length us, event | category | flops | bytes accessed | tf_op | source)
XLA Modules:
  0.0 68.5 jit_solution(9972218874655897815)
XLA Ops:
  1.9 65.1 %shard_map.85 = (f32[1,24]{1,0:T(1,128)}, f32[64,192]{1,0:T(8,128)}, f32[24,512]{1,0:T(8,128)}) custom-call(bf16[64,192]{1,0:T(8,128)(2,1)} %bitcast.3, bf16[192,1280]{1,0:T(8,128)(2,1)} %xt_ref.1, bf16[24,512]{1,0:T(8,128)(2,1)} %ts_ref.1, bf16[24,1280]{1,0:T(8,128)(2,1)} %tt_ref.1, f32[1]{0:T(128)S(6)} %copy.9.ss_ref, f32[1]{0:T(128)S(6)} %copy.10.st_ref), custom_call_target="tpu_custom_call" | custom-call | tf_op jit(solution)/shard_map/pallas_call | solution.py:650
  67.1 1.5 %shard_map.86 = (f32[1,24]{1,0:T(1,128)}, f32[64,192]{1,0:T(8,128)}, f32[24,512]{1,0:T(8,128)}) custom-call(f32[1,24]{1,0:T(1,128)} %get-tuple-element.9.loss_ref, f32[64,192]{1,0:T(8,128)} %get-tuple-element.10.image_ref, f32[24,512]{1,0:T(8,128)} %get-tuple-element.11.text_ref), custom_call_target="tpu_custom_call" | custom-call | tf_op jit(solution)/shard_map/pallas_call | solution.py:711

commit v5 on v4

--- a/solution.py
+++ b/solution.py
@@ -25,12 +25,12 @@
     )
 
 
-def loop(low, high, body):
+def loop(low, high, body, unroll=False):
     def step(i, carry):
         body(i)
         return carry
 
-    lax.fori_loop(low, high, step, 0)
+    lax.fori_loop(low, high, step, 0, unroll=unroll)
 
 
 def join_lse(parts):
@@ -269,7 +269,7 @@
             lanes = pl.ds(pl.multiple_of(c * 2 * rows + k2 * 128, 128), 128)
             img_s[at, lanes] = part.astype(BF16)
 
-    loop(0, 2 * tn, unpack)
+    loop(0, 2 * tn, unpack, True)
     both_far = img_t.at[pl.ds(pl.multiple_of(far * rows, mid), 2 * rows)]
     teach(1, both_far, both_far, sibling).wait_recv()
 
@@ -318,14 +318,14 @@
 
         if last:
             text_wait(0, 0, half - 1)
-        loop(first, end, join_a)
+        loop(first, end, join_a, True)
         sc_s[part, :] = (
             lax.dot_general(text_s[part, :], img_s[...], NN, preferred_element_type=F32) * factor_s
         )
         if last:
             sc_t[part, :] = teacher(0, wa)
             text_wait(1, 0, half - 1)
-        loop(first, end, join_b)
+        loop(first, end, join_b, True)
         if last:
             sc_t[part, :] = (sc_t[part, :] + teacher(wa, wc)) * factor_t
         else:
@@ -357,7 +357,7 @@
             )
 
         none = jnp.full((8, images), -jnp.inf, F32)
-        peaks = lax.fori_loop(first, end, columns, (none, none))
+        peaks = lax.fori_loop(first, end, columns, (none, none), unroll=True)
         row_ps = jnp.max(peaks[0], 0, keepdims=True)
         row_pt = jnp.max(peaks[1], 0, keepdims=True)
 
@@ -375,7 +375,7 @@
             )
 
         zero = jnp.zeros((8, images), F32)
-        sums = lax.fori_loop(first, end, by_rows, (zero, zero, zero))
+        sums = lax.fori_loop(first, end, by_rows, (zero, zero, zero), unroll=True)
         return [row_ps, row_pt] + [jnp.sum(v, 0, keepdims=True) for v in sums]
 
     def ring_place(j):
@@ -395,7 +395,7 @@
         across = colstat[...].T
         cbuf[zn - 1] = across[0:2]
         cmean[zn - 1] = across[2:3]
-        loop(0, zn - 1, lambda j: c_copy(j).start())
+        loop(0, zn - 1, lambda j: c_copy(j).start(), True)
 
     cuts = [0, 4, 6, 8]
     text_step(5)
@@ -443,9 +443,9 @@
         device = at_chip(dx, dy, core)
         return remote(rmean.at[sn - 1], rmean.at[m], send.at[10], recv.at[10], device)
 
-    loop(0, sn - 1, lambda m: r_copy(m).start())
-    loop(0, zn - 1, lambda j: cm_copy(j).start())
-    loop(0, sn - 1, lambda m: rm_copy(m).start())
+    loop(0, sn - 1, lambda m: r_copy(m).start(), True)
+    loop(0, zn - 1, lambda j: cm_copy(j).start(), True)
+    loop(0, sn - 1, lambda m: rm_copy(m).start(), True)
     text_tr[...] = text_s[...].astype(F32).T.astype(BF16)
 
     whole_of(rbuf, 3, sn - 1).wait_recv()
@@ -468,7 +468,7 @@
             g = e_rs[at, :] * row_fs - e_rt[at, :] * row_ft + e_cs[at, :] * fs - e_ct[at, :] * ft
             g_ref[at, :] = g.astype(BF16)
 
-        loop(cuts[k], cuts[k + 1], grads)
+        loop(cuts[k], cuts[k + 1], grads, True)
 
     def text_part(first, end):
         at = pl.ds(first * tile, (end - first) * tile)
@@ -541,12 +541,12 @@
             out[k, pl.ds(wx, wx // 2), :] = rest.astype(BF16)
 
     image_part(1 - core)
-    loop(0, tn, lambda t2: pack(sstage, None, t2))
+    loop(0, tn, lambda t2: pack(sstage, None, t2), True)
     i_sib = remote(sstage, sland, send.at[7], recv.at[7], sibling)
     i_sib.start()
     image_part(core)
     i_sib.wait_recv()
-    loop(0, tn, lambda t2: pack(istage, sland, t2))
+    loop(0, tn, lambda t2: pack(istage, sland, t2), True)
 
     def i_copy(m):
         dx, dy = chip_at(m)
@@ -556,7 +556,7 @@
         ]
         return remote(src, iland.at[m], send.at[8], recv.at[8], at_chip(dx, dy, core))
 
-    loop(0, sn - 1, lambda m: i_copy(m).start())
+    loop(0, sn - 1, lambda m: i_copy(m).start(), True)
 
     whole_of(hland, 4, len(relays)).wait_recv()
     whole_of(oland, 9, 2).wait_recv()

time: 68.7 us -> 66.4 us (0.967)
  Pallas kernels: 66.6 us -> 64.3 us
    pallas_call x1, Pallas kernels: 65.1 us -> 62.8 us  [body(): pl.pallas_call(functools.partial(kernel, zn, tn), out_shape=(jax.ShapeDty...]
where the time goes in v5:
time: 66.4 us; the launch traced here: 66.2 us
  Pallas kernels  64.3 us (97%)
  between operations  1.93 us (3%)
    pallas_call x1, Pallas kernels, body(): pl.pallas_call(functools.partial(kernel, zn, tn), out_shape=(jax.ShapeDty...  62.8 us
    pallas_call x1, Pallas kernels, body(): pl.pallas_call(deliver, out_shape=[jax.ShapeDtypeStruct(v.shape, F32) for...  1.49 us

profile of v5, /device:TPU:1, one launch (start us, length us, event | category | flops | bytes accessed | tf_op | source)
XLA Modules:
  0.0 66.2 jit_solution(15364073441554246545)
XLA Ops:
  1.9 62.8 %shard_map.85 = (f32[1,24]{1,0:T(1,128)}, f32[64,192]{1,0:T(8,128)}, f32[24,512]{1,0:T(8,128)}) custom-call(bf16[64,192]{1,0:T(8,128)(2,1)} %bitcast.3, bf16[192,1280]{1,0:T(8,128)(2,1)} %xt_ref.1, bf16[24,512]{1,0:T(8,128)(2,1)} %ts_ref.1, bf16[24,1280]{1,0:T(8,128)(2,1)} %tt_ref.1, f32[1]{0:T(128)S(6)} %copy.9.ss_ref, f32[1]{0:T(128)S(6)} %copy.10.st_ref), custom_call_target="tpu_custom_call" | custom-call | tf_op jit(solution)/shard_map/pallas_call | solution.py:650
  64.7 1.5 %shard_map.86 = (f32[1,24]{1,0:T(1,128)}, f32[64,192]{1,0:T(8,128)}, f32[24,512]{1,0:T(8,128)}) custom-call(f32[1,24]{1,0:T(1,128)} %get-tuple-element.9.loss_ref, f32[64,192]{1,0:T(8,128)} %get-tuple-element.10.image_ref, f32[24,512]{1,0:T(8,128)} %get-tuple-element.11.text_ref), custom_call_target="tpu_custom_call" | custom-call | tf_op jit(solution)/shard_map/pallas_call | solution.py:711

commit v6 on v5

--- a/solution.py
+++ b/solution.py
@@ -452,7 +452,7 @@
     row_lse = join_lse([rbuf[k] for k in range(sn)])
     whole_of(cbuf, 0, zn - 1).wait_recv()
     col_lse = join_lse([cbuf[k] for k in range(zn)])
-    colback[...] = jnp.concatenate([col_lse, jnp.zeros((126, texts), F32)], 0).T
+    colback[...] = jnp.concatenate([col_lse, jnp.zeros((6, texts), F32)], 0).T
 
     def grad_tiles(k):
         row_fs = 0.5 * jnp.exp(stats[k][0] - row_lse[0:1])
@@ -480,11 +480,11 @@
         return 2 * (half - 1) if d == half else 2 * (d - 1) + (1 if way == 0 else 0)
 
     def hop(way, d):
-        return ring(d if way == 0 else zn - d)
+        return ring(d % zn if way == 0 else (zn - d) % zn)
 
     quarter = half // 2
-    relays = [(w, d) for d in range(quarter - 1, 0, -1) for w in range(2)]
-    directs = relays
+    relays = [(w, d) for d in range(quarter - 1, 0, -1) for w in range(2)] + [(0, -1), (1, -1)]
+    directs = [(w, d) for d in range(quarter - 2, 0, -1) for w in range(2)]
     wg = ws // 2
 
     def h_copy(k):
@@ -509,15 +509,15 @@
     for way in range(2):
         ostage[way] = q_ref[place(way, half), :, way * wg : (way + 1) * wg].astype(BF16)
         o_copy(way).start()
-    for k, (way, d) in enumerate(relays):
+    def to_relay(k):
+        way, d = relays[k]
         hstage[k] = q_ref[place(way, d + quarter)].astype(BF16)
         h_copy(k).start()
+
+    for k in range(len(relays) - 2):
+        to_relay(k)
     grad_tiles(0)
 
-    text_part(0, quarter)
-    for k, (way, d) in enumerate(directs):
-        dstage[k] = q_ref[place(way, d)].astype(BF16)
-        d_copy(k).start()
 
     def image_part(c):
         at = pl.ds(pl.multiple_of(c * 2 * rows, 128), 2 * rows)
@@ -544,6 +544,12 @@
     loop(0, tn, lambda t2: pack(sstage, None, t2), True)
     i_sib = remote(sstage, sland, send.at[7], recv.at[7], sibling)
     i_sib.start()
+    text_part(0, quarter)
+    to_relay(len(relays) - 2)
+    to_relay(len(relays) - 1)
+    for k, (way, d) in enumerate(directs):
+        dstage[k] = q_ref[place(way, d)].astype(BF16)
+        d_copy(k).start()
     image_part(core)
     i_sib.wait_recv()
     loop(0, tn, lambda t2: pack(istage, sland, t2), True)
@@ -677,14 +683,14 @@
             pltpu.VMEM((zn, 1, texts), F32),
             pltpu.VMEM((sn, 2, images), F32),
             pltpu.VMEM((sn, 1, images), F32),
-            pltpu.VMEM((texts, 128), F32),
+            pltpu.VMEM((texts, 8), F32),
             pltpu.VMEM((texts, images), BF16),
             pltpu.VMEM((zn, pairs, ws), F32),
             pltpu.VMEM((ws, 2 * rows), F32),
-            pltpu.VMEM((half - 2, pairs, ws), BF16),
-            pltpu.VMEM((half - 2, pairs, ws), BF16),
-            pltpu.VMEM((half - 2, pairs, ws), BF16),
-            pltpu.VMEM((half - 2, pairs, ws), BF16),
+            pltpu.VMEM((half - 4, pairs, ws), BF16),
+            pltpu.VMEM((half - 4, pairs, ws), BF16),
+            pltpu.VMEM((half, pairs, ws), BF16),
+            pltpu.VMEM((half, pairs, ws), BF16),
             pltpu.VMEM((2, pairs, ws // 2), BF16),
             pltpu.VMEM((2, pairs, ws // 2), BF16),
             pltpu.VMEM((2, pairs, ws), BF16),

time: 66.4 us -> 66.5 us (level)
  no operation moved by 1% of the time
where the time goes in v6:
time: 66.5 us; the launch traced here: 66.3 us
  Pallas kernels  64.4 us (97%)
  between operations  1.93 us (3%)
    pallas_call x1, Pallas kernels, body(): pl.pallas_call(functools.partial(kernel, zn, tn), out_shape=(jax.ShapeDty...  62.9 us
    pallas_call x1, Pallas kernels, body(): pl.pallas_call(deliver, out_shape=[jax.ShapeDtypeStruct(v.shape, F32) for...  1.49 us

profile of v6, /device:TPU:1, one launch (start us, length us, event | category | flops | bytes accessed | tf_op | source)
XLA Modules:
  0.0 66.3 jit_solution(976939750267789648)
XLA Ops:
  1.9 62.9 %shard_map.85 = (f32[1,24]{1,0:T(1,128)}, f32[64,192]{1,0:T(8,128)}, f32[24,512]{1,0:T(8,128)}) custom-call(bf16[64,192]{1,0:T(8,128)(2,1)} %bitcast.3, bf16[192,1280]{1,0:T(8,128)(2,1)} %xt_ref.1, bf16[24,512]{1,0:T(8,128)(2,1)} %ts_ref.1, bf16[24,1280]{1,0:T(8,128)(2,1)} %tt_ref.1, f32[1]{0:T(128)S(6)} %copy.9.ss_ref, f32[1]{0:T(128)S(6)} %copy.10.st_ref), custom_call_target="tpu_custom_call" | custom-call | tf_op jit(solution)/shard_map/pallas_call | solution.py:656
  64.9 1.5 %shard_map.86 = (f32[1,24]{1,0:T(1,128)}, f32[64,192]{1,0:T(8,128)}, f32[24,512]{1,0:T(8,128)}) custom-call(f32[1,24]{1,0:T(1,128)} %get-tuple-element.9.loss_ref, f32[64,192]{1,0:T(8,128)} %get-tuple-element.10.image_ref, f32[24,512]{1,0:T(8,128)} %get-tuple-element.11.text_ref), custom_call_target="tpu_custom_call" | custom-call | tf_op jit(solution)/shard_map/pallas_call | solution.py:717
